TPU v7x, 128 devices: a whole 4x4x4 slice. The times are simulated.
128 devices in a mesh: row: 8 (over x, z_hi), col: 16 (over z_lo, y, core).
Axes of the slice: x: 4, y: 4, z: 4 (z_hi: 2, z_lo: 2; z = z_hi * 2 + z_lo), core: 2. Of those that a mesh axis runs over, the one named last changes fastest.
Arguments:
- activations: bfloat16 [2048, 16384], P(('row', 'col')), may hold values from -6 to 6
- labels: int32 [2048], P(('row', 'col')), may hold values from 0 to 63
- valid: int32 [2048], P(('row', 'col')), may hold values 0 or 1
- class_weight: float32 [64], replicated, may hold values from 0.25 to 4
Outputs:
- gram: float32 [16384, 16384], P('row', 'col')
- class_means: float32 [64, 16384], P(None, ('row', 'col'))
All inputs are finite; a program needn't handle non-finite values. No bound on the sum of `valid` on one device may be relied on, other than what follows from the above.
Results may differ from a plain program's by a relative error of at most 0.0028.
Values may be sent and summed in bfloat16 or wider, within the bound.
A program may use at most 128 MiB of HBM per device.

v0:
```python
import jax
import jax.numpy as jnp
from jax import lax
from jax.sharding import PartitionSpec as P


def over_rows(left, right):
    return lax.dot_general(
        left, right, (((0,), (0,)), ((), ())), preferred_element_type=jnp.float32
    )


def body(activations, labels, valid, class_weight):
    n_row = lax.axis_size("row")
    n_col = lax.axis_size("col")
    tok = activations.shape[0]
    width = activations.shape[1]
    classes = class_weight.shape[0]
    col_width = width // n_col
    all_labels, all_valid = (
        lax.all_gather(labels, ("row", "col"), axis=0, tiled=True),
        lax.all_gather(valid, ("row", "col"), axis=0, tiled=True),
    )
    total = all_labels.shape[0]
    onehot = (all_labels[:, None] == jnp.arange(classes, dtype=jnp.int32)[None, :]).astype(
        jnp.float32
    )
    kept = onehot * all_valid.astype(jnp.float32)[:, None]
    weights = jnp.dot(kept, class_weight, precision=lax.Precision.HIGHEST)
    counts = jnp.sum(kept, axis=0)
    grouped_col = lax.all_to_all(activations, "col", split_axis=1, concat_axis=0, tiled=True)
    grouped_row = lax.all_to_all(activations, "row", split_axis=1, concat_axis=0, tiled=True)
    panel = lax.all_gather(grouped_col, "row", axis=0, tiled=True)
    scaled = (weights[:, None] * panel).astype(jnp.bfloat16)
    scaled_four = scaled.reshape(n_row, n_col, tok, col_width)
    piece = lax.all_gather(grouped_row, "col", axis=0, tiled=True)
    group = n_row * tok
    count = piece.shape[0] // group
    partner = scaled_four
    partner = partner.transpose(1, 0, 2, 3).reshape(count * group, col_width)
    gram_acc = over_rows(piece, partner)
    local_hot = (labels[:, None] == jnp.arange(classes, dtype=jnp.int32)[None, :]).astype(
        jnp.float32
    )
    local_kept = (local_hot * valid.astype(jnp.float32)[:, None]).astype(jnp.bfloat16)
    partial_sums = over_rows(local_kept, activations)
    sums = lax.psum_scatter(partial_sums, ("row", "col"), scatter_dimension=1, tiled=True)
    gram = gram_acc / float(total)
    class_means = sums / (counts[:, None] + 1.0)
    return (gram, class_means)


def solution(mesh):
    in_specs = (P(("row", "col"), None), P(("row", "col")), P(("row", "col")), P())
    out_specs = (P("row", "col"), P(None, ("row", "col")))
    return jax.shard_map(body, mesh=mesh, in_specs=in_specs, out_specs=out_specs, check_vma=False)
```

profile of v0, /device:TPU:1, one launch (start us, length us, event | category | flops | bytes accessed | tf_op | source)
XLA Modules:
  0.0 716.6 jit_solution(17773324407665934596)
XLA Ops:
  8.0 0.0 copy-start
  8.0 0.0 copy-start.1
  8.0 0.0 copy-start.3
  8.0 0.0 copy-start.2
  8.0 0.0 all-gather.3.cloned.1.call-start
  8.1 1.1 copy.26
  9.2 17.1 %all_to_all.38 = bf16[16,16,1024]{2,0,1:T(8,128)(2,1)} all-to-all(bf16[16,16,1024]{2,0,1:T(8,128)(2,1)S(1)} %bitcast.33), channel_id=1, replica_groups=mesh['row'=8,'col'=16] {'col'}, dimensions={1} | all-to-all | bytes 1048576 | tf_op jit(solution)/shard_map/all_to_all | solution.py:31
  26.3 0.0 all-gather.3.cloned.1.call-update
  26.4 0.0 reduce-scatter.2.cloned.1.call-start
  26.4 0.7 convert_element_type.20
  27.1 3.8 fusion.5
  30.9 0.0 reduce-scatter.2.cloned.1.call-update
  30.9 0.0 all-gather.5.cloned.1.call-start
  31.0 0.0 copy-done.1
  31.0 19.7 %all_to_all.39 = bf16[16,8,2048]{2,0,1:T(8,128)(2,1)} all-to-all(bf16[16,8,2048]{2,0,1:T(8,128)(2,1)S(1)} %bitcast.34), channel_id=1, replica_groups=mesh['row'=8,'col'=16] {'row'}, dimensions={1} | all-to-all | bytes 1048576 | tf_op jit(solution)/shard_map/all_to_all | solution.py:32
  50.7 0.0 all-gather.5.cloned.1.call-update
  50.7 0.0 copy-done.3
  50.7 0.3 dynamic-update-slice.1
  51.0 0.0 copy-done.2
  51.0 0.3 dynamic-update-slice
  51.3 74.5 %all-reduce.2 = (s32[2048]{0:T(1024)S(1)}, s32[2048]{0:T(1024)S(1)}) all-reduce(s32[2048]{0:T(1024)S(1)} %dynamic-update-slice.1, s32[2048]{0:T(1024)S(1)} %dynamic-update-slice), channel_id=1, replica_groups=mesh['row'=8,'col'=16] {'row','col'}, use_global_device_ids=true, to_apply=%add.1 | all-reduce | flops 4096 | bytes 32768
  125.8 0.2 select_reduce_fusion
  125.9 0.0 copy-done
  125.9 0.4 fusion
  126.4 0.0 all-gather.3.cloned.1.call-done
  126.4 3.0 multiply_convert_fusion
  129.4 2.5 copy.18
  131.9 552.0 %reduce-scatter.2.cloned.1.call-done = f32[64,128]{1,0:T(8,128)} async-done(((f32[64,16384]{1,0:T(8,128)}), f32[64,128]{1,0:T(8,128)}) %reduce-scatter.2.cloned.1.call-update) | async-done | bytes 32784 | tf_op jit(solution)/shard_map/reduce_scatter | solution.py:47
  683.9 1.5 broadcast_divide_fusion
  685.4 0.0 all-gather.5.cloned.1.call-done
  685.4 14.5 %multiply_bitcast_fusion = f32[2048,1024]{0,1:T(8,128)} fusion(bf16[2048,1024]{1,0:T(8,128)(2,1)} %bitcast.30, bf16[2048,2048]{1,0:T(8,128)(2,1)} %all-gather.5.cloned.1.call-done), kind=kOutput, calls=%fused_computation | convolution fusion | flops 8592031744 | bytes 20971520 | tf_op jit(solution)/shard_map/dot_general | solution.py:8
  699.9 9.2 %copy.20 = f32[2048,1024]{1,0:T(8,128)} copy(f32[2048,1024]{0,1:T(8,128)} %multiply_bitcast_fusion) | data formatting | bytes 16777216
  (5 shorter events, 0.1 us)
Async XLA Ops:
  8.0 117.9 %copy-start = (f32[64]{0:T(128)S(1)}, f32[64]{0:T(128)}, u32[]{:S(2)}) copy-start(f32[64]{0:T(128)} %param.7) | copy-start | bytes 772
  8.0 22.9 %copy-start.1 = (bf16[16,16384]{1,0:T(8,128)(2,1)S(1)}, bf16[16,16384]{1,0:T(8,128)(2,1)}, u32[]{:S(2)}) copy-start(bf16[16,16384]{1,0:T(8,128)(2,1)} %param.4) | copy-start | bytes 1572868
  8.0 42.7 %copy-start.3 = (s32[16]{0:T(128)S(1)}, s32[16]{0:T(128)}, u32[]{:S(2)}) copy-start(s32[16]{0:T(128)} %param.6) | copy-start | bytes 196
  8.0 43.0 %copy-start.2 = (s32[16]{0:T(128)S(1)}, s32[16]{0:T(128)}, u32[]{:S(2)}) copy-start(s32[16]{0:T(128)} %param.5) | copy-start | bytes 196
  8.0 118.3 %all-gather.3.cloned.1.call-start = ((), (), s32[]{:S(2)}) async-start(), calls=%async_computation.3 | async-start | bytes 4718592 | tf_op jit(solution)/shard_map/all_gather | solution.py:33
  26.4 657.6 %reduce-scatter.2.cloned.1.call-start = ((), (), s32[]{:S(2)}) async-start(), calls=%async_computation.5 | async-start | bytes 4227072 | tf_op jit(solution)/shard_map/reduce_scatter | solution.py:47
  30.9 654.5 %all-gather.5.cloned.1.call-start = ((), (), s32[]{:S(2)}) async-start(), calls=%async_computation.4 | async-start | bytes 8912896 | tf_op jit(solution)/shard_map/all_gather | solution.py:36
Sparse Core Ops, SparseCore 0:
  26.5 77.5 all-gather.2
  105.8 51.5 all-gather.4
Sparse Core Ops, SparseCore 1:
  31.0 652.9 reduce-scatter.1
where the time goes:
time: 719 us; the launch traced here: 717 us
  waiting for transfers between devices  552 us (77%)
  blocking collectives  111 us (15%)
  matrix products  18.8 us (3%)
  between operations  15.6 us (2%)
  local copies, waits for them, and re-layouts  13.4 us (2%)
    reduce_scatter x1, waiting for transfers between devices, body(): lax.psum_scatter(partial_sums, ('row', 'col'), scatter_dimension=1, tiled...  552 us
    unnamed x1, blocking collectives  74.5 us
    all_to_all x1, blocking collectives, body(): lax.all_to_all(activations, 'row', split_axis=1, concat_axis=0, tiled=True)  19.7 us
    dot_general x2, matrix products, over_rows(): lax.dot_general(left, right, (((0,), (0,)), ((), ())), preferred_element_...  18.3 us
    all_to_all x1, blocking collectives, body(): lax.all_to_all(activations, 'col', split_axis=1, concat_axis=0, tiled=True)  17.1 us
  transfers between devices with their start and end apart: 3, of which 1 were waited for; matrix products, arithmetic and copies ran while one was open for 2% of the time, Pallas kernels for 0%

commit v1 on v0

v1 whole, which is shorter than its diff:
```python
import jax
import jax.numpy as jnp
from jax import lax
from jax.experimental import pallas as pl
from jax.experimental.pallas import tpu as pltpu
from jax.sharding import PartitionSpec as P

MESH = pl.DeviceIdType.MESH

OFF = (0, 1, 3, 2)
NEG = (0, 2, 1, 3)
UPWARD = (0, 3)


def pair(px, py, core, zl):
    return ((px * 4 + py) * 2 + core) * 2 + zl


def kernel(x_ref, lab_ref, val_ref, cw_ref, gram_ref, means_ref, xs, rp, cp, sc, sums, send, recv, local):
    tok, width = x_ref.shape
    block = width // 8
    half = block // 2
    row, col = lax.axis_index("row"), lax.axis_index("col")
    x, zh = row // 2, row % 2
    zl, y, core = col // 8, (col // 2) % 4, col % 2

    def flip(v, by):
        return (1 - v) if by else v

    def device(ox=0, oy=0, ozh=0, ozl=0, ok=0):
        r = ((x + ox) % 4) * 2 + flip(zh, ozh)
        c = (flip(zl, ozl) * 4 + (y + oy) % 4) * 2 + flip(core, ok)
        return r, c

    stage = [
        pltpu.make_async_copy(
            x_ref.at[:, pl.ds(b * block, block)], xs.at[b, :, pl.ds(0, block)], local.at[b]
        )
        for b in range(8)
    ]
    for s in stage:
        s.start()

    row_peers = [(p, ozh) for p in range(4) for ozh in range(2) if (p, ozh) != (0, 0)]
    col_peers = [
        (p, ozl, ok)
        for p in range(4)
        for ozl in range(2)
        for ok in range(2)
        if (p, ozl, ok) != (0, 0, 0)
    ]
    barrier = pltpu.get_barrier_semaphore()
    for p, ozh in row_peers:
        pl.semaphore_signal(barrier, inc=1, device_id=device(ox=OFF[p], ozh=ozh), device_id_type=MESH)
    for p, ozl, ok in col_peers:
        pl.semaphore_signal(
            barrier, inc=1, device_id=device(oy=OFF[p], ozl=ozl, ok=ok), device_id_type=MESH
        )

    diag = lax.broadcasted_iota(jnp.int32, (tok, tok), 0) == lax.broadcasted_iota(
        jnp.int32, (tok, tok), 1
    )
    lab = jnp.sum(jnp.where(diag, lab_ref[...].astype(jnp.float32), 0.0), axis=1, keepdims=True)
    val = jnp.sum(jnp.where(diag, val_ref[...].astype(jnp.float32), 0.0), axis=1, keepdims=True)
    lanes = lax.broadcasted_iota(jnp.int32, (tok, 128), 1).astype(jnp.float32)
    kept = jnp.where(lanes == lab, val, 0.0).astype(jnp.bfloat16)
    for b in range(8):
        xs[b, :, block:] = kept
    for s in stage:
        s.wait()
    pl.semaphore_wait(barrier, len(row_peers) + len(col_peers))

    copies = {}

    def go(name, src, dst, to):
        i = len(copies)
        copies[name] = pltpu.make_async_remote_copy(
            src_ref=src,
            dst_ref=dst,
            send_sem=send.at[i],
            recv_sem=recv.at[i],
            device_id=to,
            device_id_type=MESH,
        )
        copies[name].start()

    own_r = pltpu.make_async_copy(xs.at[row], rp.at[0, 0], local.at[0])
    own_r.start()
    own_c = pltpu.make_async_copy(
        xs.at[col // 2, :, pl.ds(pl.multiple_of(core * half, half), half)], cp.at[0, 0], local.at[1]
    )
    own_c.start()

    def first_r(p, ozh):
        r, c = device(ox=OFF[p], ozh=ozh)
        go(("r", p, ozh), xs.at[r], rp.at[pair(NEG[p], 0, 0, 0), ozh], (r, c))

    def first_c(p, ozl, ok):
        r, c = device(oy=OFF[p], ozl=ozl, ok=ok)
        go(
            ("c", p, ozl, ok),
            xs.at[c // 2, :, pl.ds(pl.multiple_of((c % 2) * half, half), half)],
            cp.at[pair(0, NEG[p], ok, ozl), 0],
            (r, c),
        )

    for p in range(4):
        for ozh in range(2):
            if (p, ozh) in row_peers:
                first_r(p, ozh)
        for ozl in range(2):
            for ok in range(2):
                if (p, ozl, ok) in col_peers:
                    first_c(p, ozl, ok)
    own_r.wait()
    own_c.wait()

    def r_of(px, py, q):
        return rp.at[pair(px, py, 0, q)]

    def c_of(px, py, q):
        return cp.at[pl.ds(pair(px, py, 0, 0), 4), q]

    def ring_r(px, q):
        go(("ru", px, q), r_of(px, 0, q), r_of(px, 2, q), device(oy=1))
        go(("rd", px, q), r_of(px, 0, q), r_of(px, 1, q), device(oy=3))

    def ring_c(py, q):
        go(("cu", py, q), c_of(0, py, q), c_of(2, py, q), device(ox=1))
        go(("cd", py, q), c_of(0, py, q), c_of(1, py, q), device(ox=3))

    def twin(px, py):
        two = pl.ds(pair(px, py, 0, 0), 2)
        go(("t", px, py), rp.at[two], rp.at[pl.ds(pair(px, py, 1, 0), 2)], device(ok=1))

    for p in range(4):
        for ozh in range(2):
            if (p, ozh) in row_peers:
                copies["r", NEG[p], ozh].wait_recv()
        go(("rz", p), r_of(p, 0, 0), r_of(p, 0, 1), device(ozl=1))
        ring_r(p, 0)
        for ozl in range(2):
            for ok in range(2):
                if (p, ozl, ok) in col_peers:
                    copies["c", NEG[p], ozl, ok].wait_recv()
        go(("cz", p), c_of(0, p, 0), c_of(0, p, 1), device(ozh=1))
        ring_c(p, 0)
    for p in range(4):
        copies["rz", p].wait_recv()
        ring_r(p, 1)
        twin(p, 0)
        copies["cz", p].wait_recv()
        ring_c(p, 1)

    for q in range(2):
        for p in range(4):
            copies["ru", p, q].wait_recv()
            if p in UPWARD:
                go(("rf", p, q), r_of(p, 2, q), r_of(p, 3, q), device(oy=1))
            copies["cu", p, q].wait_recv()
            if p in UPWARD:
                go(("cf", p, q), c_of(2, p, q), c_of(3, p, q), device(ox=1))
            copies["rd", p, q].wait_recv()
            if p not in UPWARD:
                go(("rf", p, q), r_of(p, 1, q), r_of(p, 3, q), device(oy=3))
            copies["cd", p, q].wait_recv()
            if p not in UPWARD:
                go(("cf", p, q), c_of(1, p, q), c_of(3, p, q), device(ox=3))
            if q == 1:
                twin(p, 1)
                twin(p, 2)

    tile = 256
    lane = pl.multiple_of(col * 128, 128)

    def multiply(px, py, n):
        start, n = pair(px, py, 0, 0), n * 4
        rows = n * 2 * tok
        first = (px, py) == (0, 0)
        pairs = pl.ds(start, n)
        k = rp[pairs, :, :, block:].reshape(rows, 128)
        w = jnp.sum(k[:, :64].astype(jnp.float32) * cw_ref[...], axis=1, keepdims=True)
        sc[:rows, :] = (w * cp[pairs].reshape(rows, half).astype(jnp.float32)).astype(jnp.bfloat16)
        mine = rp[pairs, :, :, pl.ds(lane, 128)].reshape(rows, 128)
        both = jnp.concatenate([mine, jnp.ones((rows, 128), jnp.bfloat16)], axis=1)
        part = over_rows(k, both)
        if first:
            sums[...] = part
        else:
            sums[...] += part

        @pl.loop(0, block // tile)
        def _(i):
            at = pl.ds(pl.multiple_of(i * tile, tile), tile)
            part = over_rows(rp[pairs, :, :, at].reshape(rows, tile), sc[:rows, :])
            if first:
                gram_ref[at, :] = part
            else:
                gram_ref[at, :] += part

    for px in range(3):
        for py in range(3):
            copies["t", px, py].wait_recv()
        multiply(px, 0, 3)
    for p in range(4):
        for q in range(2):
            copies["rf", p, q].wait_recv()
        twin(p, 3)
    for py in range(3):
        copies["t", 3, py].wait_recv()
        for q in range(2):
            copies["cf", py, q].wait_recv()
    multiply(3, 0, 3)
    for px in range(3):
        copies["t", px, 3].wait_recv()
        multiply(px, 3, 1)
    copies["t", 3, 3].wait_recv()
    for q in range(2):
        copies["cf", 3, q].wait_recv()
    multiply(3, 3, 1)
    means_ref[...] = sums[:64, :128] / (sums[:64, 128:] + 1.0)
    for c in copies.values():
        c.wait_send()


def over_rows(left, right):
    return lax.dot_general(
        left, right, (((0,), (0,)), ((), ())), preferred_element_type=jnp.float32
    )


def body(activations, labels, valid, class_weight):
    tok, width = activations.shape
    total = tok * lax.axis_size("row") * lax.axis_size("col")
    classes = class_weight.shape[0]
    block = width // 8
    vmem = pl.BlockSpec(memory_space=pltpu.VMEM)
    gram, means = pl.pallas_call(
        kernel,
        out_shape=(
            pltpu.VMEM((block, block // 2), jnp.float32),
            jax.ShapeDtypeStruct((classes, 128), jnp.float32),
        ),
        in_specs=[pl.BlockSpec(memory_space=pl.ANY), vmem, vmem, vmem],
        out_specs=(vmem, vmem),
        scratch_shapes=[
            pltpu.VMEM((8, tok, block + 128), jnp.bfloat16),
            pltpu.VMEM((64, 2, tok, block + 128), jnp.bfloat16),
            pltpu.VMEM((64, 2, tok, block // 2), jnp.bfloat16),
            pltpu.VMEM((512, block // 2), jnp.bfloat16),
            pltpu.VMEM((128, 256), jnp.float32),
            pltpu.SemaphoreType.DMA((96,)),
            pltpu.SemaphoreType.DMA((96,)),
            pltpu.SemaphoreType.DMA((8,)),
        ],
        compiler_params=pltpu.CompilerParams(
            collective_id=0, has_side_effects=True, vmem_limit_bytes=40 * 1024 * 1024
        ),
    )(
        activations,
        labels.reshape(1, tok),
        valid.reshape(1, tok),
        class_weight.reshape(1, classes),
    )
    return gram / float(total), means


def solution(mesh):
    in_specs = (P(("row", "col"), None), P(("row", "col")), P(("row", "col")), P())
    out_specs = (P("row", "col"), P(None, ("row", "col")))
    return jax.shard_map(body, mesh=mesh, in_specs=in_specs, out_specs=out_specs, check_vma=False)
```

time: 719 us -> 89.7 us (0.12)
  waiting for transfers between devices: 552 us -> 0 us
  blocking collectives: 111 us -> 0 us
  Pallas kernels: 0 us -> 79.4 us
  matrix products: 18.8 us -> 0 us
  between operations: 15.6 us -> 0.65 us
  local copies, waits for them, and re-layouts: 13.4 us -> 3.61 us
    reduce_scatter x1 -> x0, waiting for transfers between devices: 552 us -> none  [body(): lax.psum_scatter(partial_sums, ('row', 'col'), scatter_dimension=1, tiled...]
    pallas_call x0 -> x1, Pallas kernels: none -> 79.4 us  [body(): pl.pallas_call(kernel, out_shape=(pltpu.VMEM((block, block // 2), jnp.flo...]
    unnamed x1 -> x0, blocking collectives: 74.5 us -> none
    all_to_all x2 -> x0, blocking collectives: 36.8 us -> none  [the longest x1 19.7 us: body(): lax.all_to_all(activations, 'row', split_axis=1, concat_axis=0, tiled=True)]
    dot_general x3 -> x0, matrix products: 18.8 us -> none  [the longest x2 18.3 us: over_rows(): lax.dot_general(left, right, (((0,), (0,)), ((), ())), preferred_element_...]
  transfers between devices with their start and end apart: 3 -> 0, of which waited for: 1 -> 0; matrix products, arithmetic and copies ran while one was open for 2% -> 0% of each run, Pallas kernels for 0% -> 0%
where the time goes in v1:
time: 89.7 us; the launch traced here: 88 us
  Pallas kernels  79.4 us (89%)
  other arithmetic  4.38 us (5%)
  local copies, waits for them, and re-layouts  3.61 us (4%)
    pallas_call x1, Pallas kernels, body(): pl.pallas_call(kernel, out_shape=(pltpu.VMEM((block, block // 2), jnp.flo...  79.4 us
    div x1, other arithmetic, body(): return (gram / float(total), means)  4.38 us
    unnamed x9, local copies, waits for them, and re-layouts  3.61 us

profile of v1, /device:TPU:1, one launch (start us, length us, event | category | flops | bytes accessed | tf_op | source)
XLA Modules:
  0.0 88.0 jit_solution(16948102254252126348)
XLA Ops:
  0.6 0.0 copy-start
  0.6 1.0 %copy-done = bf16[16,16384]{1,0:T(8,128)(2,1)S(1)} copy-done((bf16[16,16384]{1,0:T(8,128)(2,1)S(1)}, bf16[16,16384]{1,0:T(8,128)(2,1)}, u32[]{:S(2)}) %copy-start) | copy-done | bytes 524312
  1.7 0.0 copy-start.1
  1.7 0.7 copy-done.1
  2.3 0.0 copy-start.2
  2.3 0.7 copy-done.2
  3.0 0.0 copy-start.3
  3.0 0.7 copy-done.3
  3.6 79.4 %shard_map.59 = (f32[2048,1024]{1,0:T(8,128)S(1)}, f32[64,128]{1,0:T(8,128)S(1)}) custom-call(bf16[16,16384]{1,0:T(8,128)(2,1)S(1)} %copy-done, s32[1,16]{1,0:T(1,128)S(1)} %bitcast.3, s32[1,16]{1,0:T(1,128)S(1)} %bitcast.4, f32[1,64]{1,0:T(1,128)S(1)} %bitcast.5), custom_call_target="tpu_custom_call" | custom-call | tf_op jit(solution)/shard_map/pallas_call | solution.py:238
  83.0 4.4 %broadcast_multiply_fusion = f32[2048,1024]{1,0:T(8,128)} fusion(f32[2048,1024]{1,0:T(8,128)S(1)} %get-tuple-element.4), kind=kLoop, calls=%fused_computation | loop fusion | flops 2097152 | bytes 16777216 | tf_op jit(solution)/shard_map/div | solution.py:265
  87.4 0.6 copy.7
Async XLA Ops:
  0.6 1.0 %copy-start = (bf16[16,16384]{1,0:T(8,128)(2,1)S(1)}, bf16[16,16384]{1,0:T(8,128)(2,1)}, u32[]{:S(2)}) copy-start(bf16[16,16384]{1,0:T(8,128)(2,1)} %x_ref.1) | copy-start | bytes 1572868
  1.7 0.7 copy-start.1
  2.3 0.7 copy-start.2
  3.0 0.7 copy-start.3

commit v2 on v0

v2 whole, which is shorter than its diff:
```python
import jax
import jax.numpy as jnp
from jax import lax
from jax.experimental import pallas as pl
from jax.experimental.pallas import tpu as pltpu
from jax.sharding import PartitionSpec as P

MESH = pl.DeviceIdType.MESH

OFF = (0, 1, 3, 2)
NEG = (0, 2, 1, 3)
UPWARD = (0, 3)
EARLY = (((0, 0), (0, 1)), ((0, 2), (1, 0)))
MIDDLE = (((2, 0), (1, 1)), ((1, 2), (2, 1)))
LATE = (((2, 2), (0, 3)), ((3, 0), (1, 3)))
LAST = ((3, 1), (2, 3), (3, 2), (3, 3))


def over_rows(left, right):
    return lax.dot_general(
        left, right, (((0,), (0,)), ((), ())), preferred_element_type=jnp.float32
    )


def at_group(px, py):
    return px * 4 + py


def rows_of(ref, groups, lanes):
    parts = [ref[at_group(*g), :, :, :, lanes] for g in groups]
    parts = [p.reshape(-1, p.shape[-1]) for p in parts]
    return parts[0] if len(parts) == 1 else jnp.concatenate(parts, axis=0)


def class_sums(rp, groups, block, lane):
    kept = rows_of(rp, groups, pl.ds(block, 128))
    mine = rows_of(rp, groups, pl.ds(lane, 128))
    both = jnp.concatenate([mine, jnp.ones(mine.shape, jnp.bfloat16)], axis=1)
    return kept, over_rows(kept, both)


def exchange(
    x_hbm, lab_hbm, val_hbm, cw_hbm, acc, sums, rp, last, xs, cp, tb, sc, lab_ref, val_ref, cw_ref, send, recv, local
):
    tok, width = x_hbm.shape
    block = width // 8
    half = block // 2
    row, col = lax.axis_index("row"), lax.axis_index("col")
    x, zh = row // 2, row % 2
    zl, y, core = col // 8, (col // 2) % 4, col % 2

    def flip(v, by):
        return (1 - v) if by else v

    def device(ox=0, oy=0, ozh=0, ozl=0, ok=0):
        r = ((x + ox) % 4) * 2 + flip(zh, ozh)
        c = (flip(zl, ozl) * 4 + (y + oy) % 4) * 2 + flip(core, ok)
        return r, c

    stage = [
        pltpu.make_async_copy(
            x_hbm.at[:, pl.ds(b * block, block)], xs.at[b, :, pl.ds(0, block)], local.at[b]
        )
        for b in range(8)
    ]
    small = [
        pltpu.make_async_copy(s, d, local.at[8 + i])
        for i, (s, d) in enumerate(((lab_hbm, lab_ref), (val_hbm, val_ref), (cw_hbm, cw_ref)))
    ]
    for s in small + stage:
        s.start()

    row_peers = [(p, h) for p in range(4) for h in range(2) if (p, h) != (0, 0)]
    col_peers = [(p, ok) for p in range(4) for ok in range(2) if (p, ok) != (0, 0)]
    peers = (
        [device(ox=OFF[p], ozh=h, ozl=h) for p, h in row_peers]
        + [device(oy=OFF[p], ok=ok) for p, ok in col_peers]
        + [device(ozl=1), device(ozh=1)]
    )
    barrier = pltpu.get_barrier_semaphore()
    for peer in peers:
        pl.semaphore_signal(barrier, inc=1, device_id=peer, device_id_type=MESH)

    for s in small:
        s.wait()
    diag = lax.broadcasted_iota(jnp.int32, (tok, tok), 0) == lax.broadcasted_iota(
        jnp.int32, (tok, tok), 1
    )
    lab = jnp.sum(jnp.where(diag, lab_ref[...].astype(jnp.float32), 0.0), axis=1, keepdims=True)
    val = jnp.sum(jnp.where(diag, val_ref[...].astype(jnp.float32), 0.0), axis=1, keepdims=True)
    lanes = lax.broadcasted_iota(jnp.int32, (tok, 128), 1).astype(jnp.float32)
    kept = jnp.where(lanes == lab, val, 0.0).astype(jnp.bfloat16)
    for b in range(8):
        xs[b, :, block:] = kept
    for s in stage:
        s.wait()
    own = [
        pltpu.make_async_copy(xs.at[row], rp.at[0, 0, 0], local.at[0]),
        pltpu.make_async_copy(
            xs.at[zl * 4 + y, :, pl.ds(pl.multiple_of(core * half, half), half)],
            cp.at[0, 0, 0],
            local.at[1],
        ),
        pltpu.make_async_copy(
            xs.at[(1 - zl) * 4 + y, :, pl.ds(pl.multiple_of(core * half, half), half)],
            tb.at[0, 0],
            local.at[2],
        ),
    ]
    for s in own:
        s.start()
    pl.semaphore_wait(barrier, len(peers))

    copies = {}

    def go(name, src, dst, to):
        i = len(copies)
        copies[name] = pltpu.make_async_remote_copy(
            src_ref=src,
            dst_ref=dst,
            send_sem=send.at[i],
            recv_sem=recv.at[i],
            device_id=to,
            device_id_type=MESH,
        )
        copies[name].start()

    def got(*names):
        for n in names:
            copies[n].wait_recv()

    for p in range(4):
        for h in (1, 0):
            if (p, h) in row_peers:
                to = device(ox=OFF[p], ozh=h, ozl=h)
                go(("r", p, h), xs.at[to[0]], rp.at[at_group(NEG[p], 0), 0, h], to)
        for ok in range(2):
            if (p, ok) in col_peers:
                r, c = device(oy=OFF[p], ok=ok)
                lane = pl.ds(pl.multiple_of((c % 2) * half, half), half)
                y_to = (y + OFF[p]) % 4
                go(("cs", p, ok), xs.at[zl * 4 + y_to, :, lane], cp.at[at_group(0, NEG[p]), ok, 0], (r, c))
                go(("cf", p, ok), xs.at[(1 - zl) * 4 + y_to, :, lane], tb.at[NEG[p], ok], (r, c))
    for s in own:
        s.wait()

    def r_of(px, py, q):
        return rp.at[at_group(px, py), 0, pl.ds(2 * q, 2)]

    def c_of(px, py, q):
        return cp.at[at_group(px, py), :, pl.ds(2 * q, 2)]

    def ring_r(px, q):
        go(("ru", px, q), r_of(px, 0, q), r_of(px, 2, q), device(oy=1))
        go(("rd", px, q), r_of(px, 0, q), r_of(px, 1, q), device(oy=3))

    def ring_c(py, q):
        go(("cu", py, q), c_of(0, py, q), c_of(2, py, q), device(ox=1))
        go(("cd", py, q), c_of(0, py, q), c_of(1, py, q), device(ox=3))

    def twin(px, py):
        g = at_group(px, py)
        go(("t", px, py), rp.at[g, 0], rp.at[g, 1], device(ok=1))

    for p in range(4):
        got(*[("r", NEG[p], h) for h in range(2) if (p, h) in row_peers])
        go(("rz", p), r_of(p, 0, 0), r_of(p, 0, 1), device(ozl=1))
        ring_r(p, 0)
        got(*[(n, NEG[p], ok) for n in ("cs", "cf") for ok in range(2) if (p, ok) in col_peers])
        g = at_group(0, p)
        go(("z1", p), tb.at[p], cp.at[g, :, 1], device(ozh=1, ozl=1))
        go(("z2", p), tb.at[p], cp.at[g, :, 2], device(ozl=1))
        go(("z3", p), cp.at[g, :, 0], cp.at[g, :, 3], device(ozh=1))
    for p in range(4):
        got(("z1", p))
        ring_c(p, 0)
        got(("rz", p))
        ring_r(p, 1)
        twin(p, 0)
    for p in range(4):
        got(("z2", p), ("z3", p))
        ring_c(p, 1)

    lane = pl.multiple_of(col * 128, 128)

    def weigh(groups, into, at):
        kept, part = class_sums(rp, groups, block, lane)
        w = jnp.sum(kept[:, :64].astype(jnp.float32) * cw_ref[...], axis=1, keepdims=True)
        right = rows_of(cp, groups, slice(None)).astype(jnp.float32)
        into[at, :] = (w * right).astype(jnp.bfloat16)
        return part

    def multiply(groups, first=False):
        rows = len(groups) * 8 * tok
        part = weigh(groups, sc, pl.ds(0, rows))
        if first:
            sums[...] = part
        else:
            sums[...] += part

        @pl.loop(0, 2)
        def _(i):
            at = pl.ds(pl.multiple_of(i * half, half), half)
            left = rows_of(rp, groups, at)
            for j in range(half // 256):
                to = pl.ds(j * 256, 256)
                part = over_rows(left, sc[:rows, to])
                if first:
                    acc[at, to] = part
                else:
                    acc[at, to] += part

    def ring_step(q, p):
        got(("ru", p, q), ("rd", p, q))
        if p in UPWARD:
            go(("rf", p, q), r_of(p, 2, q), r_of(p, 3, q), device(oy=1))
        else:
            go(("rf", p, q), r_of(p, 1, q), r_of(p, 3, q), device(oy=3))
        got(("cu", p, q), ("cd", p, q))
        if p in UPWARD:
            go(("cx", p, q), c_of(2, p, q), c_of(3, p, q), device(ox=1))
        else:
            go(("cx", p, q), c_of(1, p, q), c_of(3, p, q), device(ox=3))
        if q == 1:
            twin(p, 1)
            twin(p, 2)

    def ring_end(p):
        got(("rf", p, 0), ("rf", p, 1))
        twin(p, 3)
        got(("cx", p, 0), ("cx", p, 1))

    for p in range(4):
        ring_step(0, p)
    ring_step(1, 0)
    got(*[("t", px, 0) for px in range(4)], ("t", 0, 1), ("t", 0, 2))
    multiply(EARLY[0], True)
    ring_step(1, 1)
    multiply(EARLY[1])
    ring_step(1, 2)
    got(("t", 1, 1), ("t", 1, 2), ("t", 2, 1), ("t", 2, 2))
    multiply(MIDDLE[0])
    ring_step(1, 3)
    multiply(MIDDLE[1])
    ring_end(0)
    got(("t", 0, 3))
    multiply(LATE[0])
    ring_end(1)
    got(("t", 1, 3))
    multiply(LATE[1])
    ring_end(2)
    ring_end(3)
    got(("t", 2, 3), ("t", 3, 3), ("t", 3, 1), ("t", 3, 2))
    for i, g in enumerate(LAST):
        sums[...] += weigh([g], last, pl.ds(i * 8 * tok, 8 * tok))
    for c in copies.values():
        c.wait_send()


def finish(acc, sums, rp, last, gram_hbm, means, out, sems):
    rows, half = acc.shape
    total = 16 * 8 * rp.shape[3]
    writes = []
    for i in range(2):
        at = pl.ds(i * half, half)
        left = rows_of(rp, LAST, at)
        for j in range(half // 256):
            to = pl.ds(j * 256, 256)
            out[at, to] = (acc[at, to] + over_rows(left, last[:, to])) / float(total)
            n = len(writes)
            writes.append(pltpu.make_async_copy(out.at[at, to], gram_hbm.at[at, to], sems.at[n]))
            writes[n].start()
    means[...] = sums[:64, :128] / (sums[:64, 128:] + 1.0)
    for w in writes:
        w.wait()


def body(activations, labels, valid, class_weight):
    tok, width = activations.shape
    classes = class_weight.shape[0]
    block = width // 8
    half = block // 2
    vmem = pl.BlockSpec(memory_space=pltpu.VMEM)
    hbm = pl.BlockSpec(memory_space=pltpu.HBM)
    parts = pl.pallas_call(
        exchange,
        out_shape=(
            pltpu.VMEM((block, half), jnp.float32),
            pltpu.VMEM((128, 256), jnp.float32),
            pltpu.VMEM((16, 2, 4, tok, block + 128), jnp.bfloat16),
            pltpu.VMEM((len(LAST) * 8 * tok, half), jnp.bfloat16),
        ),
        in_specs=[hbm] * 4,
        out_specs=(vmem,) * 4,
        scratch_shapes=[
            pltpu.VMEM((8, tok, block + 128), jnp.bfloat16),
            pltpu.VMEM((16, 2, 4, tok, half), jnp.bfloat16),
            pltpu.VMEM((4, 2, tok, half), jnp.bfloat16),
            pltpu.VMEM((2 * 8 * tok, half), jnp.bfloat16),
            pltpu.VMEM((1, tok), jnp.int32),
            pltpu.VMEM((1, tok), jnp.int32),
            pltpu.VMEM((1, classes), jnp.float32),
            pltpu.SemaphoreType.DMA((101,)),
            pltpu.SemaphoreType.DMA((101,)),
            pltpu.SemaphoreType.DMA((11,)),
        ],
        compiler_params=pltpu.CompilerParams(
            collective_id=0, has_side_effects=True, vmem_limit_bytes=12 * 1024 * 1024
        ),
    )(
        *[
            pltpu.with_memory_space_constraint(a, pltpu.HBM)
            for a in (
                activations,
                labels.reshape(1, tok),
                valid.reshape(1, tok),
                class_weight.reshape(1, classes),
            )
        ]
    )
    return pl.pallas_call(
        finish,
        out_shape=(
            jax.ShapeDtypeStruct((block, half), jnp.float32),
            jax.ShapeDtypeStruct((classes, 128), jnp.float32),
        ),
        in_specs=[vmem] * 4,
        out_specs=(hbm, vmem),
        scratch_shapes=[pltpu.VMEM((block, half), jnp.float32), pltpu.SemaphoreType.DMA((8,))],
        compiler_params=pltpu.CompilerParams(vmem_limit_bytes=14 * 1024 * 1024),
    )(*parts)


def solution(mesh):
    in_specs = (P(("row", "col"), None), P(("row", "col")), P(("row", "col")), P())
    out_specs = (P("row", "col"), P(None, ("row", "col")))
    return jax.shard_map(body, mesh=mesh, in_specs=in_specs, out_specs=out_specs, check_vma=False)
```

time: 719 us -> 74.6 us (0.10)
  waiting for transfers between devices: 552 us -> 0 us
  blocking collectives: 111 us -> 0 us
  Pallas kernels: 0 us -> 73.8 us
  matrix products: 18.8 us -> 0 us
  between operations: 15.6 us -> 0.64 us
  local copies, waits for them, and re-layouts: 13.4 us -> 0 us
    reduce_scatter x1 -> x0, waiting for transfers between devices: 552 us -> none  [body(): lax.psum_scatter(partial_sums, ('row', 'col'), scatter_dimension=1, tiled...]
    unnamed x1 -> x0, blocking collectives: 74.5 us -> none
    pallas_call x0 -> x2, Pallas kernels: none -> 73.8 us  [the longest x1 69.1 us: body(): pl.pallas_call(exchange, out_shape=(pltpu.VMEM((block, half), jnp.float32...]
    all_to_all x2 -> x0, blocking collectives: 36.8 us -> none  [the longest x1 19.7 us: body(): lax.all_to_all(activations, 'row', split_axis=1, concat_axis=0, tiled=True)]
    dot_general x3 -> x0, matrix products: 18.8 us -> none  [the longest x2 18.3 us: over_rows(): lax.dot_general(left, right, (((0,), (0,)), ((), ())), preferred_element_...]
    unnamed x13 -> x0, local copies, waits for them, and re-layouts: 9.82 us -> none
  transfers between devices with their start and end apart: 3 -> 0, of which waited for: 1 -> 0; matrix products, arithmetic and copies ran while one was open for 2% -> 0% of each run, Pallas kernels for 0% -> 0%
where the time goes in v2:
time: 74.6 us; the launch traced here: 74.5 us
  Pallas kernels  73.8 us (99%)
    pallas_call x1, Pallas kernels, body(): pl.pallas_call(exchange, out_shape=(pltpu.VMEM((block, half), jnp.float32...  69.1 us
    pallas_call x1, Pallas kernels, body(): pl.pallas_call(finish, out_shape=(jax.ShapeDtypeStruct((block, half), jnp...  4.75 us

profile of v2, /device:TPU:1, one launch (start us, length us, event | category | flops | bytes accessed | tf_op | source)
XLA Modules:
  0.0 74.5 jit_solution(9474702726818815687)
XLA Ops:
  0.6 69.1 %shard_map.59 = (f32[2048,1024]{1,0:T(8,128)S(1)}, f32[128,256]{1,0:T(8,128)S(1)}, bf16[16,2,4,16,2176]{4,3,2,1,0:T(8,128)(2,1)S(1)}, bf16[512,1024]{1,0:T(8,128)(2,1)S(1)}) custom-call(bf16[16,16384]{1,0:T(8,128)(2,1)} %x_hbm.1, s32[1,16]{1,0:T(1,128)} %bitcast.3, s32[1,16]{1,0:T(1,128)} %bitcast.4, f32[1,64]{1,0:T(1,128)} %bitcast.5), custom_call_target="tpu_custom_call" | custom-call | tf_op jit(solution)/shard_map/pallas_call | solution.py:285
  69.7 4.8 %shard_map.60 = (f32[2048,1024]{1,0:T(8,128)}, f32[64,128]{1,0:T(8,128)}) custom-call(f32[2048,1024]{1,0:T(8,128)S(1)} %get-tuple-element.6.acc, f32[128,256]{1,0:T(8,128)S(1)} %get-tuple-element.7.sums, bf16[16,2,4,16,2176]{4,3,2,1,0:T(8,128)(2,1)S(1)} %get-tuple-element.8.rp, bf16[512,1024]{1,0:T(8,128)(2,1)S(1)} %get-tuple-element.9.last), custom_call_target="tpu_custom_call" | custom-call | tf_op jit(solution)/shard_map/pallas_call | solution.py:321

commit v3 on v0

v3 whole, which is shorter than its diff:
```python
import jax
import jax.numpy as jnp
from jax import lax
from jax.experimental import pallas as pl
from jax.experimental.pallas import tpu as pltpu
from jax.sharding import PartitionSpec as P

MESH = pl.DeviceIdType.MESH

OFF = (0, 1, 3, 2)
NEG = (0, 2, 1, 3)
UPWARD = (0, 3)
PARTS = ((0, 1), (1, 1), (2, 2))
HALVES = ((0, 2), (2, 2))
PARTS_OF = ((0, 1), (2,))
CHUNKS = (
    ((0, 0, 0, 4), (0, 1, 0, 4)),
    ((0, 2, 0, 4), (1, 0, 0, 4)),
    ((2, 0, 0, 4), (1, 1, 0, 4)),
    ((1, 2, 0, 4), (2, 1, 0, 4)),
    ((2, 2, 0, 4), (0, 3, 0, 4)),
    ((3, 0, 0, 4), (1, 3, 0, 4)),
    ((3, 1, 0, 4), (2, 3, 0, 2), (3, 2, 0, 2)),
)
LAST = ((3, 3, 0, 4), (2, 3, 2, 2), (3, 2, 2, 2))


ORDER = tuple(
    tuple(int(v) if v.isdigit() else v for v in step.split())
    for step in (
        "c 3 1 1", "c 0 1 1", "c 0 1 0", "c 2 1 1", "r 1 1", "c 1 0 1", "c 1 0 0", "c 3 0 0", "rz 0 0",
        "r 1 0", "r 0 1", "k1", "cu 0 0", "c 2 0 0", "z3 0", "c 2 0 1", "r 2 0", "z2 0", "ru 0 0",
        "c 1 1 0", "z1 0", "c 3 1 0", "r 3 0", "rd 0 0", "r 3 1", "c 2 1 0", "c 1 1 1", "r 2 1", "ru 0 1",
        "rd 1 0", "rz 0 1", "rd 1 1", "cd 1 0", "z1 2", "ru 2 0", "rz 1 0", "rz 1 1", "cu 0 2", "c 3 0 1",
        "k2", "rd 2 0", "cd 0 0", "ru 3 0", "cu 0 1", "cd 0 2", "z2 1", "rd 0 1", "cd 0 1", "ru 0 2",
        "z3 1", "z1 1", "cd 2 0", "cd 2 1", "cu 1 0", "rd 1 2", "rd 2 1", "rf 0 0", "z3 3", "z2 2",
        "rz 2 1", "t 1 0", "z3 2", "cx 0 1", "t 0 2", "k3", "z2 3", "z1 3", "rd 0 2", "rz 2 0", "rf 0 1",
        "cx 0 0", "t 0 0", "rz 3 1", "cd 1 2", "ru 1 0", "cu 2 1", "ru 3 1", "cu 1 2", "ru 2 1", "rz 3 0",
        "rf 1 0", "cu 3 0", "cd 1 1", "ru 1 2", "cd 3 0", "rf 2 0", "rf 1 1", "cd 3 1", "m 1", "t 0 3 0",
        "cd 3 2", "cu 3 2", "rd 2 2", "cu 2 0", "t 0 1", "t 2 0", "rd 3 2", "cx 1 0", "ru 2 2", "ru 3 2",
        "cd 2 2", "cu 3 1", "cx 1 1", "t 0 3 1", "t 1 3 0", "ru 1 1", "m 0", "cu 1 1", "cu 2 2", "cx 2 0",
        "rd 3 1", "t 1 1", "t 1 3 1", "t 2 3 0", "t 3 0", "t 2 2", "rf 3 0", "cx 3 1", "m 2", "rd 3 0",
        "m 5", "t 1 2", "t 3 2", "cx 3 0", "rf 2 1", "t 2 1", "rf 3 1", "cx 2 1", "m 4", "t 3 1", "t 3 3 0",
        "m 3", "t 2 3 1", "t 3 3 1", "m 6",
    )
)


def of_row(px, i):
    if i == 2:
        return [("rz", px, 0), ("rz", px, 1)]
    return [] if (px, i) == (0, 0) else [("r", px, i)]


def of_column(py, i):
    if i == 0:
        return [("c", py, ok, 0) for ok in range(2) if (py, ok) != (0, 0)]
    return [("z1", py)] if i == 1 else [("z2", py), ("z3", py)]


def row_half(px, py, q):
    if py == 0:
        return [n for i in PARTS_OF[q] for n in of_row(px, i)]
    if py == 3:
        return [("rf", px, q)]
    return [("rd" if py == 1 else "ru", px, i) for i in PARTS_OF[q]]


def column_half(px, py, q):
    if px == 0:
        return [n for i in PARTS_OF[q] for n in of_column(py, i)]
    if px == 3:
        return [("cx", py, q)]
    return [("cd" if px == 1 else "cu", py, i) for i in PARTS_OF[q]]


def product_needs(parts):
    out = ["k3"]
    for px, py, e, n in parts:
        for q in range(2):
            if e <= 2 * q < e + n:
                out += row_half(px, py, q) + column_half(px, py, q)
                out.append(("t", px, py, q) if py == 3 else ("t", px, py))
    return out


def over_rows(left, right):
    return lax.dot_general(
        left, right, (((0,), (0,)), ((), ())), preferred_element_type=jnp.float32
    )


def at_group(px, py):
    return px * 4 + py


def rows_of(ref, parts, lanes):
    out = [ref[at_group(px, py), :, pl.ds(e, n), :, lanes] for px, py, e, n in parts]
    return jnp.concatenate([p.reshape(-1, p.shape[-1]) for p in out], axis=0)


def exchange(
    x_hbm, lab_hbm, val_hbm, cw_hbm, acc, sums, rp, last, cp, tb, sc, xs, codes, lab_ref, val_ref, cw_ref, send, recv, local
):
    tok, width = x_hbm.shape
    block = width // 8
    half = block // 2
    row, col = lax.axis_index("row"), lax.axis_index("col")
    x, zh = row // 2, row % 2
    zl, y, core = col // 8, (col // 2) % 4, col % 2

    def flip(v, by):
        return (1 - v) if by else v

    def device(ox=0, oy=0, ozh=0, ozl=0, ok=0):
        r = ((x + ox) % 4) * 2 + flip(zh, ozh)
        c = (flip(zl, ozl) * 4 + (y + oy) % 4) * 2 + flip(core, ok)
        return r, c

    row_peers = [(p, h) for p in range(4) for h in range(2) if (p, h) != (0, 0)]
    col_peers = [(p, ok) for p in range(4) for ok in range(2) if (p, ok) != (0, 0)]
    peers = (
        [device(ox=OFF[p], ozh=h, ozl=h) for p, h in row_peers]
        + [device(oy=OFF[p], ok=ok) for p, ok in col_peers]
        + [device(ozl=1), device(ozh=1)]
    )
    barrier = pltpu.get_barrier_semaphore()
    for peer in peers:
        pl.semaphore_signal(barrier, inc=1, device_id=peer, device_id_type=MESH)

    stage = pltpu.make_async_copy(x_hbm, xs, local.at[6])

    def row_block(src, r):
        return src.at[:, pl.ds(pl.multiple_of(r * block, block), block)]

    def col_block(src, zl, y, core):
        return src.at[:, pl.ds(pl.multiple_of(((zl * 4 + y) * 2 + core) * half, half), half)]

    own = [
        pltpu.make_async_copy(s, d, local.at[i])
        for i, (s, d) in enumerate(
            (
                (lab_hbm, lab_ref),
                (val_hbm, val_ref),
                (cw_hbm, cw_ref),
                (row_block(x_hbm, row), rp.at[0, 0, 0]),
                (col_block(x_hbm, zl, y, core), cp.at[0, 0, 0]),
                (col_block(x_hbm, 1 - zl, y, core), tb.at[0, 0]),
            )
        )
    ]
    for s in own:
        s.start()
    for s in own[:2]:
        s.wait()
    codes[0, 0, 0, 0] = jnp.zeros((1, 128), jnp.float32)
    codes[0, 0, 0, 0, :, :tok] = (val_ref[...] * (lab_ref[...] + 1) - 1).astype(jnp.float32)
    for s in own[2:]:
        s.wait()
    pl.semaphore_wait(barrier, len(peers))

    copies = {}

    def go(name, src, dst, to):
        i = len(copies)
        copies[name] = pltpu.make_async_remote_copy(
            src_ref=src,
            dst_ref=dst,
            send_sem=send.at[i],
            recv_sem=recv.at[i],
            device_id=to,
            device_id_type=MESH,
        )
        copies[name].start()

    seen = set()

    def got(names):
        for n in names:
            if n not in seen:
                seen.add(n)
                copies[n].wait_recv()

    def r_at(px, py, part):
        return rp.at[at_group(px, py), 0, pl.ds(*part)]

    def c_at(px, py, part):
        return cp.at[at_group(px, py), :, pl.ds(*part)]

    def r_at(px, py, part):
        return rp.at[at_group(px, py), 0, pl.ds(*part)]

    def c_at(px, py, part):
        return cp.at[at_group(px, py), :, pl.ds(*part)]

    def step(kind, *at):
        name = (kind, *at)
        if kind == "r":
            px, h = at
            to = device(ox=OFF[NEG[px]], ozh=h, ozl=h)
            go(name, row_block(x_hbm, to[0]), rp.at[at_group(px, 0), 0, h], to)
        elif kind == "c":
            py, ok, other = at
            oy = OFF[NEG[py]]
            src = col_block(x_hbm, flip(zl, other), (y + oy) % 4, flip(core, ok))
            dst = tb.at[py, ok] if other else cp.at[at_group(0, py), ok, 0]
            go(name, src, dst, device(oy=oy, ok=ok))
        elif kind == "rz":
            px, h = at
            got(of_row(px, h))
            go(name, r_at(px, 0, (h, 1)), r_at(px, 0, (2 + h, 1)), device(ozl=1))
        elif kind in ("z1", "z2"):
            (py,) = at
            got([("c", py, ok, 1) for ok in range(2) if (py, ok) != (0, 0)])
            e = 1 if kind == "z1" else 2
            go(name, tb.at[py], cp.at[at_group(0, py), :, e], device(ozl=1, ozh=2 - e))
        elif kind == "z3":
            g = at_group(0, at[0])
            got(of_column(at[0], 0))
            go(name, cp.at[g, :, 0], cp.at[g, :, 3], device(ozh=1))
        elif kind in ("ru", "rd"):
            px, i = at
            got(of_row(px, i))
            py, oy = (2, 1) if kind == "ru" else (1, 3)
            go(name, r_at(px, 0, PARTS[i]), r_at(px, py, PARTS[i]), device(oy=oy))
        elif kind in ("cu", "cd"):
            py, i = at
            got(of_column(py, i))
            px, ox = (2, 1) if kind == "cu" else (1, 3)
            go(name, c_at(0, py, PARTS[i]), c_at(px, py, PARTS[i]), device(ox=ox))
        elif kind == "rf":
            px, q = at
            py, oy = (2, 1) if px in UPWARD else (1, 3)
            got(row_half(px, py, q))
            go(name, r_at(px, py, HALVES[q]), r_at(px, 3, HALVES[q]), device(oy=oy))
        elif kind == "cx":
            py, q = at
            px, ox = (2, 1) if py in UPWARD else (1, 3)
            got(column_half(px, py, q))
            go(name, c_at(px, py, HALVES[q]), c_at(3, py, HALVES[q]), device(ox=ox))
        elif kind == "t":
            px, py = at[:2]
            for q in at[2:] or range(2):
                got(row_half(px, py, q))
            part = pl.ds(*(HALVES[at[2]] if at[2:] else (0, 4)))
            g = at_group(px, py)
            go(name, rp.at[g, 0, part], rp.at[g, 1, part], device(ok=1))
        elif kind == "k1":
            for p, h in row_peers:
                to = device(ox=OFF[NEG[p]], ozh=h, ozl=h)
                go(("k1", p, h), codes.at[0, 0, 0, 0], codes.at[p, 0, 0, h], to)
        elif kind == "k2":
            got([("k1", p, h) for p, h in row_peers])
            for p, ok in col_peers:
                two = pl.ds(0, 2)
                to = device(oy=OFF[NEG[p]], ok=ok)
                go(("k2", p, ok), codes.at[:, 0, 0, two], codes.at[:, p, ok, two], to)
        elif kind == "k3":
            got([("k2", p, ok) for p, ok in col_peers])
            src, dst = (codes.at[:, :, :, pl.ds(e, 2)] for e in (0, 2))
            go("k3", src, dst, device(ozl=1))
        else:
            got(product_needs(CHUNKS[at[0]]))
            multiply(at[0])

    lane = pl.multiple_of(col * 128, 128)
    pick = lax.broadcasted_iota(jnp.int32, (8 * tok, 128), 1) == lax.broadcasted_iota(
        jnp.int32, (8 * tok, 128), 0
    ) % tok
    lanes = lax.broadcasted_iota(jnp.int32, (8 * tok, 128), 1).astype(jnp.float32)

    def weigh(parts, into):
        rows = [
            jnp.broadcast_to(codes[px, py, k, e + i], (tok, 128))
            for px, py, e, n in parts
            for k in range(2)
            for i in range(n)
        ]
        kept = []
        for a in range(0, len(rows), 8):
            spread = jnp.concatenate(rows[a : a + 8], axis=0)
            code = jnp.sum(jnp.where(pick, spread, 0.0), axis=1, keepdims=True)
            kept.append((lanes == code).astype(jnp.float32))
        kept = jnp.concatenate(kept, axis=0)
        w = jnp.sum(kept[:, :64] * cw_ref[...], axis=1, keepdims=True)
        into[...] = (w * rows_of(cp, parts, slice(None)).astype(jnp.float32)).astype(jnp.bfloat16)
        mine = rows_of(rp, parts, pl.ds(lane, 128))
        both = jnp.concatenate([mine, jnp.ones(mine.shape, jnp.bfloat16)], axis=1)
        return over_rows(kept.astype(jnp.bfloat16), both)

    def multiply(n):
        first = ("m",) not in seen
        seen.add(("m",))
        part = weigh(CHUNKS[n], sc)
        if first:
            sums[...] = part
        else:
            sums[...] += part

        @pl.loop(0, 2)
        def _(i):
            at = pl.ds(pl.multiple_of(i * half, half), half)
            left = rows_of(rp, CHUNKS[n], at)
            for j in range(half // 256):
                to = pl.ds(j * 256, 256)
                part = over_rows(left, sc[:, to])
                if first:
                    acc[at, to] = part
                else:
                    acc[at, to] += part

    for one in ORDER:
        step(*one)
    got(product_needs(LAST))
    sums[...] += weigh(LAST, last)
    for c in copies.values():
        c.wait_send()


def finish(acc, sums, rp, last, gram_hbm, means_hbm, out, means, sems):
    rows, half = acc.shape
    total = 16 * 8 * rp.shape[3]
    means[...] = sums[:64, :128] / (sums[:64, 128:] + 1.0)
    writes = [pltpu.make_async_copy(means, means_hbm, sems.at[0])]
    writes[0].start()
    for i in range(2):
        at = pl.ds(i * half, half)
        left = rows_of(rp, LAST, at)
        for j in range(half // 256):
            to = pl.ds(j * 256, 256)
            out[at, to] = (acc[at, to] + over_rows(left, last[:, to])) / float(total)
            n = len(writes)
            writes.append(pltpu.make_async_copy(out.at[at, to], gram_hbm.at[at, to], sems.at[n]))
            writes[n].start()
    for w in writes:
        w.wait()


def body(activations, labels, valid, class_weight):
    tok, width = activations.shape
    classes = class_weight.shape[0]
    block = width // 8
    half = block // 2
    chunk = 2 * 8 * tok
    vmem = pl.BlockSpec(memory_space=pltpu.VMEM)
    hbm = pl.BlockSpec(memory_space=pltpu.HBM)
    parts = pl.pallas_call(
        exchange,
        out_shape=(
            pltpu.VMEM((block, half), jnp.float32),
            pltpu.VMEM((128, 256), jnp.float32),
            pltpu.VMEM((16, 2, 4, tok, block), jnp.bfloat16),
            pltpu.VMEM((chunk, half), jnp.bfloat16),
        ),
        in_specs=[hbm] * 4,
        out_specs=(vmem,) * 4,
        scratch_shapes=[
            pltpu.VMEM((16, 2, 4, tok, half), jnp.bfloat16),
            pltpu.VMEM((4, 2, tok, half), jnp.bfloat16),
            pltpu.VMEM((chunk, half), jnp.bfloat16),
            pltpu.VMEM((tok, width), jnp.bfloat16),
            pltpu.VMEM((4, 4, 2, 4, 1, 128), jnp.float32),
            pltpu.VMEM((1, tok), jnp.int32),
            pltpu.VMEM((1, tok), jnp.int32),
            pltpu.VMEM((1, classes), jnp.float32),
            pltpu.SemaphoreType.DMA((160,)),
            pltpu.SemaphoreType.DMA((160,)),
            pltpu.SemaphoreType.DMA((7,)),
        ],
        compiler_params=pltpu.CompilerParams(
            collective_id=0, has_side_effects=True, vmem_limit_bytes=12 * 1024 * 1024
        ),
    )(
        *[
            pltpu.with_memory_space_constraint(a, pltpu.HBM)
            for a in (
                activations,
                labels.reshape(1, tok),
                valid.reshape(1, tok),
                class_weight.reshape(1, classes),
            )
        ]
    )
    return pl.pallas_call(
        finish,
        out_shape=(
            jax.ShapeDtypeStruct((block, half), jnp.float32),
            jax.ShapeDtypeStruct((classes, 128), jnp.float32),
        ),
        in_specs=[vmem] * 4,
        out_specs=(hbm, hbm),
        scratch_shapes=[
            pltpu.VMEM((block, half), jnp.float32),
            pltpu.VMEM((classes, 128), jnp.float32),
            pltpu.SemaphoreType.DMA((9,)),
        ],
        compiler_params=pltpu.CompilerParams(vmem_limit_bytes=14 * 1024 * 1024),
    )(*parts)


def solution(mesh):
    in_specs = (P(("row", "col"), None), P(("row", "col")), P(("row", "col")), P())
    out_specs = (P("row", "col"), P(None, ("row", "col")))
    return jax.shard_map(body, mesh=mesh, in_specs=in_specs, out_specs=out_specs, check_vma=False)
```

time: 719 us -> 61.4 us (0.09)
  waiting for transfers between devices: 552 us -> 0 us
  blocking collectives: 111 us -> 0 us
  Pallas kernels: 0 us -> 60.6 us
  matrix products: 18.8 us -> 0 us
  between operations: 15.6 us -> 0.64 us
  local copies, waits for them, and re-layouts: 13.4 us -> 0 us
    reduce_scatter x1 -> x0, waiting for transfers between devices: 552 us -> none  [body(): lax.psum_scatter(partial_sums, ('row', 'col'), scatter_dimension=1, tiled...]
    unnamed x1 -> x0, blocking collectives: 74.5 us -> none
    pallas_call x0 -> x2, Pallas kernels: none -> 60.6 us  [the longest x1 56.8 us: body(): pl.pallas_call(exchange, out_shape=(pltpu.VMEM((block, half), jnp.float32...]
    all_to_all x2 -> x0, blocking collectives: 36.8 us -> none  [the longest x1 19.7 us: body(): lax.all_to_all(activations, 'row', split_axis=1, concat_axis=0, tiled=True)]
    dot_general x3 -> x0, matrix products: 18.8 us -> none  [the longest x2 18.3 us: over_rows(): lax.dot_general(left, right, (((0,), (0,)), ((), ())), preferred_element_...]
    unnamed x13 -> x0, local copies, waits for them, and re-layouts: 9.82 us -> none
  transfers between devices with their start and end apart: 3 -> 0, of which waited for: 1 -> 0; matrix products, arithmetic and copies ran while one was open for 2% -> 0% of each run, Pallas kernels for 0% -> 0%
where the time goes in v3:
time: 61.4 us; the launch traced here: 61.3 us
  Pallas kernels  60.6 us (99%)
  between operations  0.64 us (1%)
    pallas_call x1, Pallas kernels, body(): pl.pallas_call(exchange, out_shape=(pltpu.VMEM((block, half), jnp.float32...  56.8 us
    pallas_call x1, Pallas kernels, body(): pl.pallas_call(finish, out_shape=(jax.ShapeDtypeStruct((block, half), jnp...  3.88 us

profile of v3, /device:TPU:1, one launch (start us, length us, event | category | flops | bytes accessed | tf_op | source)
XLA Modules:
  0.0 61.3 jit_solution(2273315649143845655)
XLA Ops:
  0.6 56.8 %shard_map.59 = (f32[2048,1024]{1,0:T(8,128)S(1)}, f32[128,256]{1,0:T(8,128)S(1)}, bf16[16,2,4,16,2048]{4,3,2,1,0:T(8,128)(2,1)S(1)}, bf16[256,1024]{1,0:T(8,128)(2,1)S(1)}) custom-call(bf16[16,16384]{1,0:T(8,128)(2,1)} %x_hbm.1, s32[1,16]{1,0:T(1,128)} %bitcast.3, s32[1,16]{1,0:T(1,128)} %bitcast.4, f32[1,64]{1,0:T(1,128)} %bitcast.5), custom_call_target="tpu_custom_call" | custom-call | tf_op jit(solution)/shard_map/pallas_call | solution.py:347
  57.4 3.9 %shard_map.60 = (f32[2048,1024]{1,0:T(8,128)}, f32[64,128]{1,0:T(8,128)}) custom-call(f32[2048,1024]{1,0:T(8,128)S(1)} %get-tuple-element.6.acc, f32[128,256]{1,0:T(8,128)S(1)} %get-tuple-element.7.sums, bf16[16,2,4,16,2048]{4,3,2,1,0:T(8,128)(2,1)S(1)} %get-tuple-element.8.rp, bf16[256,1024]{1,0:T(8,128)(2,1)S(1)} %get-tuple-element.9.last), custom_call_target="tpu_custom_call" | custom-call | tf_op jit(solution)/shard_map/pallas_call | solution.py:384

commit v4 on v3

--- a/solution.py
+++ b/solution.py
@@ -13,6 +13,8 @@
 PARTS = ((0, 1), (1, 1), (2, 2))
 HALVES = ((0, 2), (2, 2))
 PARTS_OF = ((0, 1), (2,))
+ROW_LATER = ()
+COLUMN_LATER = ()
 CHUNKS = (
     ((0, 0, 0, 4), (0, 1, 0, 4)),
     ((0, 2, 0, 4), (1, 0, 0, 4)),
@@ -25,63 +27,92 @@
 LAST = ((3, 3, 0, 4), (2, 3, 2, 2), (3, 2, 2, 2))
 
 
-ORDER = tuple(
-    tuple(int(v) if v.isdigit() else v for v in step.split())
-    for step in (
-        "c 3 1 1", "c 0 1 1", "c 0 1 0", "c 2 1 1", "r 1 1", "c 1 0 1", "c 1 0 0", "c 3 0 0", "rz 0 0",
-        "r 1 0", "r 0 1", "k1", "cu 0 0", "c 2 0 0", "z3 0", "c 2 0 1", "r 2 0", "z2 0", "ru 0 0",
-        "c 1 1 0", "z1 0", "c 3 1 0", "r 3 0", "rd 0 0", "r 3 1", "c 2 1 0", "c 1 1 1", "r 2 1", "ru 0 1",
-        "rd 1 0", "rz 0 1", "rd 1 1", "cd 1 0", "z1 2", "ru 2 0", "rz 1 0", "rz 1 1", "cu 0 2", "c 3 0 1",
-        "k2", "rd 2 0", "cd 0 0", "ru 3 0", "cu 0 1", "cd 0 2", "z2 1", "rd 0 1", "cd 0 1", "ru 0 2",
-        "z3 1", "z1 1", "cd 2 0", "cd 2 1", "cu 1 0", "rd 1 2", "rd 2 1", "rf 0 0", "z3 3", "z2 2",
-        "rz 2 1", "t 1 0", "z3 2", "cx 0 1", "t 0 2", "k3", "z2 3", "z1 3", "rd 0 2", "rz 2 0", "rf 0 1",
-        "cx 0 0", "t 0 0", "rz 3 1", "cd 1 2", "ru 1 0", "cu 2 1", "ru 3 1", "cu 1 2", "ru 2 1", "rz 3 0",
-        "rf 1 0", "cu 3 0", "cd 1 1", "ru 1 2", "cd 3 0", "rf 2 0", "rf 1 1", "cd 3 1", "m 1", "t 0 3 0",
-        "cd 3 2", "cu 3 2", "rd 2 2", "cu 2 0", "t 0 1", "t 2 0", "rd 3 2", "cx 1 0", "ru 2 2", "ru 3 2",
-        "cd 2 2", "cu 3 1", "cx 1 1", "t 0 3 1", "t 1 3 0", "ru 1 1", "m 0", "cu 1 1", "cu 2 2", "cx 2 0",
-        "rd 3 1", "t 1 1", "t 1 3 1", "t 2 3 0", "t 3 0", "t 2 2", "rf 3 0", "cx 3 1", "m 2", "rd 3 0",
-        "m 5", "t 1 2", "t 3 2", "cx 3 0", "rf 2 1", "t 2 1", "rf 3 1", "cx 2 1", "m 4", "t 3 1", "t 3 3 0",
-        "m 3", "t 2 3 1", "t 3 3 1", "m 6",
-    )
+KINDS = range(22)
+R, C, RZ, Z1, Z2, Z3, RU, RD, CU, CD, RF, CX, RV, T, K1, K2, K3, S2, M, OWN, READY, FAR = KINDS
+ORDER = (
+    (C, 0, 1, 1), (C, 0, 1, 0), (C, 1, 0, 1), (C, 1, 0, 0), (RZ, 0, 0), (R, 1, 0), (R, 0, 1), (C, 2, 0, 0),
+    (C, 2, 0, 1), (R, 2, 0), (RU, 0, 0), (RD, 0, 0), (S2,), (C, 3, 1, 1), (C, 2, 1, 1), (R, 1, 1),
+    (C, 3, 0, 0), (K1,), (CU, 0, 0), (Z3, 0), (Z2, 0), (C, 1, 1, 0), (Z1, 0), (C, 3, 1, 0), (R, 3, 0),
+    (R, 3, 1), (C, 2, 1, 0), (C, 1, 1, 1), (R, 2, 1), (RU, 0, 1), (RD, 1, 0), (RZ, 0, 1), (RD, 1, 1),
+    (CD, 1, 0), (Z1, 2), (RU, 2, 0), (RZ, 1, 0), (RZ, 1, 1), (CU, 0, 2), (C, 3, 0, 1), (K2,), (RD, 2, 0),
+    (CD, 0, 0), (RU, 3, 0), (CU, 0, 1), (CD, 0, 2), (Z2, 1), (RD, 0, 1), (CD, 0, 1), (RU, 0, 2), (Z3, 1),
+    (Z1, 1), (CD, 2, 0), (CD, 2, 1), (CU, 1, 0), (RD, 1, 2), (RD, 2, 1), (RF, 0, 0), (Z3, 3), (Z2, 2),
+    (RZ, 2, 1), (T, 1, 0), (Z3, 2), (CX, 0, 1), (T, 0, 2), (K3,), (Z2, 3), (Z1, 3), (RD, 0, 2), (RZ, 2, 0),
+    (RF, 0, 1), (CX, 0, 0), (T, 0, 0), (RZ, 3, 1), (CD, 1, 2), (RU, 1, 0), (CU, 2, 1), (RU, 3, 1),
+    (CU, 1, 2), (RU, 2, 1), (RZ, 3, 0), (RF, 1, 0), (CU, 3, 0), (CD, 1, 1), (RU, 1, 2), (CD, 3, 0),
+    (RF, 2, 0), (RF, 1, 1), (CD, 3, 1), (M, 1), (T, 0, 3, 0), (CD, 3, 2), (CU, 3, 2), (RD, 2, 2),
+    (CU, 2, 0), (T, 0, 1), (T, 2, 0), (RD, 3, 2), (CX, 1, 0), (RU, 2, 2), (RU, 3, 2), (CD, 2, 2),
+    (CU, 3, 1), (CX, 1, 1), (T, 0, 3, 1), (T, 1, 3, 0), (RU, 1, 1), (M, 0), (CU, 1, 1), (CU, 2, 2),
+    (CX, 2, 0), (RD, 3, 1), (T, 1, 1), (T, 1, 3, 1), (T, 2, 3, 0), (T, 3, 0), (T, 2, 2), (RF, 3, 0),
+    (CX, 3, 1), (M, 2), (RD, 3, 0), (M, 5), (T, 1, 2), (T, 3, 2), (CX, 3, 0), (RF, 2, 1), (T, 2, 1),
+    (RF, 3, 1), (CX, 2, 1), (M, 4), (T, 3, 1), (T, 3, 3, 0), (M, 3), (T, 2, 3, 1), (T, 3, 3, 1), (M, 6),
 )
+
+
+def row_ready(px, h):
+    if px == 3:
+        return [(FAR, "next") if h else (READY, "x+")]
+    return [(READY, "next")] if px and h else []
+
+
+def column_ready(py, ok):
+    if py == 3:
+        return [(FAR, "twin") if ok else (READY, "y+")]
+    return [(READY, "twin")] if py and ok else []
+
+
+def first_of_column(py, other):
+    own = [(OWN, 4 + other)] if py == 0 else []
+    return own + [(C, py, ok, other) for ok in range(2) if (py, ok) != (0, 0)]
 
 
 def of_row(px, i):
     if i == 2:
-        return [("rz", px, 0), ("rz", px, 1)]
-    return [] if (px, i) == (0, 0) else [("r", px, i)]
+        return [(RV, px, 0)] if px in ROW_LATER else [(RZ, px, 0), (RZ, px, 1)]
+    return [(OWN, 3)] if (px, i) == (0, 0) else [(R, px, i)]
 
 
 def of_column(py, i):
     if i == 0:
-        return [("c", py, ok, 0) for ok in range(2) if (py, ok) != (0, 0)]
-    return [("z1", py)] if i == 1 else [("z2", py), ("z3", py)]
+        return first_of_column(py, 0)
+    return [(Z1, py)] if i == 1 else [(Z2, py)] + ([] if py in COLUMN_LATER else [(Z3, py)])
 
 
 def row_half(px, py, q):
+    if px in ROW_LATER and q == 1:
+        return [(RV, px, py)]
     if py == 0:
         return [n for i in PARTS_OF[q] for n in of_row(px, i)]
     if py == 3:
-        return [("rf", px, q)]
-    return [("rd" if py == 1 else "ru", px, i) for i in PARTS_OF[q]]
+        return [(RF, px, q)]
+    return [(RD if py == 1 else RU, px, i) for i in PARTS_OF[q]]
+
+
+def column_ring(px, py, parts, q):
+    if px == 0:
+        return [n for i in parts for n in of_column(py, i)]
+    if px == 3:
+        return [(CX, py, q)]
+    return [(CD if px == 1 else CU, py, i) for i in parts]
 
 
 def column_half(px, py, q):
-    if px == 0:
-        return [n for i in PARTS_OF[q] for n in of_column(py, i)]
-    if px == 3:
-        return [("cx", py, q)]
-    return [("cd" if px == 1 else "cu", py, i) for i in PARTS_OF[q]]
+    later = [(Z3, py, px)] if py in COLUMN_LATER and q == 1 else []
+    return column_ring(px, py, PARTS_OF[q], q) + later
 
 
 def product_needs(parts):
-    out = ["k3"]
+    out = [(K3,)]
     for px, py, e, n in parts:
         for q in range(2):
             if e <= 2 * q < e + n:
                 out += row_half(px, py, q) + column_half(px, py, q)
-                out.append(("t", px, py, q) if py == 3 else ("t", px, py))
+                out.append((T, px, py, q) if py == 3 else (T, px, py))
     return out
+
+
+def column_part(py, i):
+    return (2, 1) if py in COLUMN_LATER and i == 2 else PARTS[i]
 
 
 def over_rows(left, right):
@@ -100,7 +131,7 @@
 
 
 def exchange(
-    x_hbm, lab_hbm, val_hbm, cw_hbm, acc, sums, rp, last, cp, tb, sc, xs, codes, lab_ref, val_ref, cw_ref, send, recv, local
+    x_hbm, lab_hbm, val_hbm, cw_hbm, acc, sums, rp, last, cp, tb, sc, codes, lab_ref, val_ref, cw_ref, send, recv, local, ready, far
 ):
     tok, width = x_hbm.shape
     block = width // 8
@@ -119,22 +150,30 @@
 
     row_peers = [(p, h) for p in range(4) for h in range(2) if (p, h) != (0, 0)]
     col_peers = [(p, ok) for p in range(4) for ok in range(2) if (p, ok) != (0, 0)]
-    peers = (
-        [device(ox=OFF[p], ozh=h, ozl=h) for p, h in row_peers]
-        + [device(oy=OFF[p], ok=ok) for p, ok in col_peers]
-        + [device(ozl=1), device(ozh=1)]
-    )
+    near = {
+        "x+": dict(ox=1),
+        "x-": dict(ox=3),
+        "y+": dict(oy=1),
+        "y-": dict(oy=3),
+        "pair": dict(ozl=1),
+        "next": dict(ozl=1, ozh=1),
+        "twin": dict(ok=1),
+    }
+    sides = list(near)
+    mirror = {"x+": "x-", "x-": "x+", "y+": "y-", "y-": "y+"}
     barrier = pltpu.get_barrier_semaphore()
-    for peer in peers:
-        pl.semaphore_signal(barrier, inc=1, device_id=peer, device_id_type=MESH)
-
-    stage = pltpu.make_async_copy(x_hbm, xs, local.at[6])
-
-    def row_block(src, r):
-        return src.at[:, pl.ds(pl.multiple_of(r * block, block), block)]
-
-    def col_block(src, zl, y, core):
-        return src.at[:, pl.ds(pl.multiple_of(((zl * 4 + y) * 2 + core) * half, half), half)]
+    for to in near.values():
+        pl.semaphore_signal(barrier, inc=1, device_id=device(**to), device_id_type=MESH)
+
+    def tell(sems, d):
+        sem = sems.at[sides.index(mirror.get(d, d))]
+        pl.semaphore_signal(sem, inc=1, device_id=device(**near[d]), device_id_type=MESH)
+
+    def row_block(r):
+        return x_hbm.at[:, pl.ds(pl.multiple_of(r * block, block), block)]
+
+    def col_block(zl, y, core):
+        return x_hbm.at[:, pl.ds(pl.multiple_of(((zl * 4 + y) * 2 + core) * half, half), half)]
 
     own = [
         pltpu.make_async_copy(s, d, local.at[i])
@@ -143,21 +182,17 @@
                 (lab_hbm, lab_ref),
                 (val_hbm, val_ref),
                 (cw_hbm, cw_ref),
-                (row_block(x_hbm, row), rp.at[0, 0, 0]),
-                (col_block(x_hbm, zl, y, core), cp.at[0, 0, 0]),
-                (col_block(x_hbm, 1 - zl, y, core), tb.at[0, 0]),
+                (row_block(row), rp.at[0, 0, 0]),
+                (col_block(zl, y, core), cp.at[0, 0, 0]),
+                (col_block(1 - zl, y, core), tb.at[0, 0]),
             )
         )
     ]
     for s in own:
         s.start()
-    for s in own[:2]:
-        s.wait()
-    codes[0, 0, 0, 0] = jnp.zeros((1, 128), jnp.float32)
-    codes[0, 0, 0, 0, :, :tok] = (val_ref[...] * (lab_ref[...] + 1) - 1).astype(jnp.float32)
-    for s in own[2:]:
-        s.wait()
-    pl.semaphore_wait(barrier, len(peers))
+    pl.semaphore_wait(barrier, len(near))
+    for d in near:
+        tell(ready, d)
 
     copies = {}
 
@@ -179,7 +214,13 @@
         for n in names:
             if n not in seen:
                 seen.add(n)
-                copies[n].wait_recv()
+                if n[0] == OWN:
+                    own[n[1]].wait()
+                elif n[0] in (READY, FAR):
+                    sems = ready if n[0] == READY else far
+                    pl.semaphore_wait(sems.at[sides.index(n[1])], 1)
+                else:
+                    copies[n].wait_recv()
 
     def r_at(px, py, part):
         return rp.at[at_group(px, py), 0, pl.ds(*part)]
@@ -195,70 +236,88 @@
 
     def step(kind, *at):
         name = (kind, *at)
-        if kind == "r":
+        if kind == R:
             px, h = at
+            got(row_ready(px, h))
             to = device(ox=OFF[NEG[px]], ozh=h, ozl=h)
-            go(name, row_block(x_hbm, to[0]), rp.at[at_group(px, 0), 0, h], to)
-        elif kind == "c":
+            go(name, row_block(to[0]), rp.at[at_group(px, 0), 0, h], to)
+        elif kind == C:
             py, ok, other = at
+            got(column_ready(py, ok))
             oy = OFF[NEG[py]]
-            src = col_block(x_hbm, flip(zl, other), (y + oy) % 4, flip(core, ok))
+            src = col_block(flip(zl, other), (y + oy) % 4, flip(core, ok))
             dst = tb.at[py, ok] if other else cp.at[at_group(0, py), ok, 0]
             go(name, src, dst, device(oy=oy, ok=ok))
-        elif kind == "rz":
+        elif kind == RZ:
             px, h = at
             got(of_row(px, h))
             go(name, r_at(px, 0, (h, 1)), r_at(px, 0, (2 + h, 1)), device(ozl=1))
-        elif kind in ("z1", "z2"):
+        elif kind == RV:
+            px, py = at
+            got(row_half(px, py, 0))
+            go(name, r_at(px, py, HALVES[0]), r_at(px, py, HALVES[1]), device(ozl=1))
+        elif kind in (Z1, Z2):
             (py,) = at
-            got([("c", py, ok, 1) for ok in range(2) if (py, ok) != (0, 0)])
-            e = 1 if kind == "z1" else 2
+            got(first_of_column(py, 1))
+            e = 1 if kind == Z1 else 2
             go(name, tb.at[py], cp.at[at_group(0, py), :, e], device(ozl=1, ozh=2 - e))
-        elif kind == "z3":
-            g = at_group(0, at[0])
-            got(of_column(at[0], 0))
+        elif kind == Z3:
+            py, px = at if len(at) == 2 else (at[0], 0)
+            g = at_group(px, py)
+            got(column_ring(px, py, (0,), 0) + [(READY, "next")])
             go(name, cp.at[g, :, 0], cp.at[g, :, 3], device(ozh=1))
-        elif kind in ("ru", "rd"):
+        elif kind in (RU, RD):
             px, i = at
             got(of_row(px, i))
-            py, oy = (2, 1) if kind == "ru" else (1, 3)
+            py, oy = (2, 1) if kind == RU else (1, 3)
             go(name, r_at(px, 0, PARTS[i]), r_at(px, py, PARTS[i]), device(oy=oy))
-        elif kind in ("cu", "cd"):
+        elif kind in (CU, CD):
             py, i = at
             got(of_column(py, i))
-            px, ox = (2, 1) if kind == "cu" else (1, 3)
-            go(name, c_at(0, py, PARTS[i]), c_at(px, py, PARTS[i]), device(ox=ox))
-        elif kind == "rf":
+            px, ox = (2, 1) if kind == CU else (1, 3)
+            part = column_part(py, i)
+            go(name, c_at(0, py, part), c_at(px, py, part), device(ox=ox))
+        elif kind == RF:
             px, q = at
             py, oy = (2, 1) if px in UPWARD else (1, 3)
             got(row_half(px, py, q))
             go(name, r_at(px, py, HALVES[q]), r_at(px, 3, HALVES[q]), device(oy=oy))
-        elif kind == "cx":
+        elif kind == CX:
             py, q = at
             px, ox = (2, 1) if py in UPWARD else (1, 3)
-            got(column_half(px, py, q))
-            go(name, c_at(px, py, HALVES[q]), c_at(3, py, HALVES[q]), device(ox=ox))
-        elif kind == "t":
+            got(column_ring(px, py, PARTS_OF[q], q))
+            part = column_part(py, 2) if q else HALVES[0]
+            go(name, c_at(px, py, part), c_at(3, py, part), device(ox=ox))
+        elif kind == T:
             px, py = at[:2]
             for q in at[2:] or range(2):
                 got(row_half(px, py, q))
             part = pl.ds(*(HALVES[at[2]] if at[2:] else (0, 4)))
             g = at_group(px, py)
             go(name, rp.at[g, 0, part], rp.at[g, 1, part], device(ok=1))
-        elif kind == "k1":
+        elif kind == S2:
+            got([(READY, "x+"), (READY, "y+")])
+            tell(far, "next")
+            tell(far, "twin")
+        elif kind == K1:
+            got([(OWN, 0), (OWN, 1)])
+            codes[0, 0, 0, 0] = jnp.zeros((1, 128), jnp.float32)
+            codes[0, 0, 0, 0, :, :tok] = (val_ref[...] * (lab_ref[...] + 1) - 1).astype(jnp.float32)
             for p, h in row_peers:
+                got(row_ready(p, h))
                 to = device(ox=OFF[NEG[p]], ozh=h, ozl=h)
-                go(("k1", p, h), codes.at[0, 0, 0, 0], codes.at[p, 0, 0, h], to)
-        elif kind == "k2":
-            got([("k1", p, h) for p, h in row_peers])
+                go((K1, p, h), codes.at[0, 0, 0, 0], codes.at[p, 0, 0, h], to)
+        elif kind == K2:
+            got([(K1, p, h) for p, h in row_peers])
             for p, ok in col_peers:
+                got(column_ready(p, ok))
                 two = pl.ds(0, 2)
                 to = device(oy=OFF[NEG[p]], ok=ok)
-                go(("k2", p, ok), codes.at[:, 0, 0, two], codes.at[:, p, ok, two], to)
-        elif kind == "k3":
-            got([("k2", p, ok) for p, ok in col_peers])
+                go((K2, p, ok), codes.at[:, 0, 0, two], codes.at[:, p, ok, two], to)
+        elif kind == K3:
+            got([(K2, p, ok) for p, ok in col_peers])
             src, dst = (codes.at[:, :, :, pl.ds(e, 2)] for e in (0, 2))
-            go("k3", src, dst, device(ozl=1))
+            go(name, src, dst, device(ozl=1))
         else:
             got(product_needs(CHUNKS[at[0]]))
             multiply(at[0])
@@ -270,6 +329,7 @@
     lanes = lax.broadcasted_iota(jnp.int32, (8 * tok, 128), 1).astype(jnp.float32)
 
     def weigh(parts, into):
+        got([(OWN, 2)])
         rows = [
             jnp.broadcast_to(codes[px, py, k, e + i], (tok, 128))
             for px, py, e, n in parts
@@ -289,8 +349,8 @@
         return over_rows(kept.astype(jnp.bfloat16), both)
 
     def multiply(n):
-        first = ("m",) not in seen
-        seen.add(("m",))
+        first = (M,) not in seen
+        seen.add((M,))
         part = weigh(CHUNKS[n], sc)
         if first:
             sums[...] = part
@@ -311,7 +371,7 @@
 
     for one in ORDER:
         step(*one)
-    got(product_needs(LAST))
+    got(product_needs(LAST) + [(READY, d) for d in near])
     sums[...] += weigh(LAST, last)
     for c in copies.values():
         c.wait_send()
@@ -358,14 +418,15 @@
             pltpu.VMEM((16, 2, 4, tok, half), jnp.bfloat16),
             pltpu.VMEM((4, 2, tok, half), jnp.bfloat16),
             pltpu.VMEM((chunk, half), jnp.bfloat16),
-            pltpu.VMEM((tok, width), jnp.bfloat16),
             pltpu.VMEM((4, 4, 2, 4, 1, 128), jnp.float32),
             pltpu.VMEM((1, tok), jnp.int32),
             pltpu.VMEM((1, tok), jnp.int32),
             pltpu.VMEM((1, classes), jnp.float32),
             pltpu.SemaphoreType.DMA((160,)),
             pltpu.SemaphoreType.DMA((160,)),
-            pltpu.SemaphoreType.DMA((7,)),
+            pltpu.SemaphoreType.DMA((6,)),
+            pltpu.SemaphoreType.REGULAR((7,)),
+            pltpu.SemaphoreType.REGULAR((7,)),
         ],
         compiler_params=pltpu.CompilerParams(
             collective_id=0, has_side_effects=True, vmem_limit_bytes=12 * 1024 * 1024

time: 61.4 us -> 60.1 us (0.979)
  Pallas kernels: 60.6 us -> 59.4 us
    pallas_call x1, Pallas kernels: 56.8 us -> 55.5 us  [body(): pl.pallas_call(exchange, out_shape=(pltpu.VMEM((block, half), jnp.float32...]
where the time goes in v4:
time: 60.1 us; the launch traced here: 60 us
  Pallas kernels  59.4 us (99%)
  between operations  0.64 us (1%)
    pallas_call x1, Pallas kernels, body(): pl.pallas_call(exchange, out_shape=(pltpu.VMEM((block, half), jnp.float32...  55.5 us
    pallas_call x1, Pallas kernels, body(): pl.pallas_call(finish, out_shape=(jax.ShapeDtypeStruct((block, half), jnp...  3.89 us

profile of v4, /device:TPU:1, one launch (start us, length us, event | category | flops | bytes accessed | tf_op | source)
XLA Modules:
  0.0 60.0 jit_solution(8405393228969952560)
XLA Ops:
  0.6 55.5 %shard_map.59 = (f32[2048,1024]{1,0:T(8,128)S(1)}, f32[128,256]{1,0:T(8,128)S(1)}, bf16[16,2,4,16,2048]{4,3,2,1,0:T(8,128)(2,1)S(1)}, bf16[256,1024]{1,0:T(8,128)(2,1)S(1)}) custom-call(bf16[16,16384]{1,0:T(8,128)(2,1)} %x_hbm.1, s32[1,16]{1,0:T(1,128)} %bitcast.3, s32[1,16]{1,0:T(1,128)} %bitcast.4, f32[1,64]{1,0:T(1,128)} %bitcast.5), custom_call_target="tpu_custom_call" | custom-call | tf_op jit(solution)/shard_map/pallas_call | solution.py:407
  56.1 3.9 %shard_map.60 = (f32[2048,1024]{1,0:T(8,128)}, f32[64,128]{1,0:T(8,128)}) custom-call(f32[2048,1024]{1,0:T(8,128)S(1)} %get-tuple-element.6.acc, f32[128,256]{1,0:T(8,128)S(1)} %get-tuple-element.7.sums, bf16[16,2,4,16,2048]{4,3,2,1,0:T(8,128)(2,1)S(1)} %get-tuple-element.8.rp, bf16[256,1024]{1,0:T(8,128)(2,1)S(1)} %get-tuple-element.9.last), custom_call_target="tpu_custom_call" | custom-call | tf_op jit(solution)/shard_map/pallas_call | solution.py:445

commit v5 on v4

--- a/solution.py
+++ b/solution.py
@@ -13,7 +13,7 @@
 PARTS = ((0, 1), (1, 1), (2, 2))
 HALVES = ((0, 2), (2, 2))
 PARTS_OF = ((0, 1), (2,))
-ROW_LATER = ()
+ROW_LATER = (0,)
 COLUMN_LATER = ()
 CHUNKS = (
     ((0, 0, 0, 4), (0, 1, 0, 4)),
@@ -30,22 +30,22 @@
 KINDS = range(22)
 R, C, RZ, Z1, Z2, Z3, RU, RD, CU, CD, RF, CX, RV, T, K1, K2, K3, S2, M, OWN, READY, FAR = KINDS
 ORDER = (
-    (C, 0, 1, 1), (C, 0, 1, 0), (C, 1, 0, 1), (C, 1, 0, 0), (RZ, 0, 0), (R, 1, 0), (R, 0, 1), (C, 2, 0, 0),
-    (C, 2, 0, 1), (R, 2, 0), (RU, 0, 0), (RD, 0, 0), (S2,), (C, 3, 1, 1), (C, 2, 1, 1), (R, 1, 1),
-    (C, 3, 0, 0), (K1,), (CU, 0, 0), (Z3, 0), (Z2, 0), (C, 1, 1, 0), (Z1, 0), (C, 3, 1, 0), (R, 3, 0),
-    (R, 3, 1), (C, 2, 1, 0), (C, 1, 1, 1), (R, 2, 1), (RU, 0, 1), (RD, 1, 0), (RZ, 0, 1), (RD, 1, 1),
-    (CD, 1, 0), (Z1, 2), (RU, 2, 0), (RZ, 1, 0), (RZ, 1, 1), (CU, 0, 2), (C, 3, 0, 1), (K2,), (RD, 2, 0),
-    (CD, 0, 0), (RU, 3, 0), (CU, 0, 1), (CD, 0, 2), (Z2, 1), (RD, 0, 1), (CD, 0, 1), (RU, 0, 2), (Z3, 1),
-    (Z1, 1), (CD, 2, 0), (CD, 2, 1), (CU, 1, 0), (RD, 1, 2), (RD, 2, 1), (RF, 0, 0), (Z3, 3), (Z2, 2),
-    (RZ, 2, 1), (T, 1, 0), (Z3, 2), (CX, 0, 1), (T, 0, 2), (K3,), (Z2, 3), (Z1, 3), (RD, 0, 2), (RZ, 2, 0),
-    (RF, 0, 1), (CX, 0, 0), (T, 0, 0), (RZ, 3, 1), (CD, 1, 2), (RU, 1, 0), (CU, 2, 1), (RU, 3, 1),
-    (CU, 1, 2), (RU, 2, 1), (RZ, 3, 0), (RF, 1, 0), (CU, 3, 0), (CD, 1, 1), (RU, 1, 2), (CD, 3, 0),
-    (RF, 2, 0), (RF, 1, 1), (CD, 3, 1), (M, 1), (T, 0, 3, 0), (CD, 3, 2), (CU, 3, 2), (RD, 2, 2),
-    (CU, 2, 0), (T, 0, 1), (T, 2, 0), (RD, 3, 2), (CX, 1, 0), (RU, 2, 2), (RU, 3, 2), (CD, 2, 2),
-    (CU, 3, 1), (CX, 1, 1), (T, 0, 3, 1), (T, 1, 3, 0), (RU, 1, 1), (M, 0), (CU, 1, 1), (CU, 2, 2),
-    (CX, 2, 0), (RD, 3, 1), (T, 1, 1), (T, 1, 3, 1), (T, 2, 3, 0), (T, 3, 0), (T, 2, 2), (RF, 3, 0),
-    (CX, 3, 1), (M, 2), (RD, 3, 0), (M, 5), (T, 1, 2), (T, 3, 2), (CX, 3, 0), (RF, 2, 1), (T, 2, 1),
-    (RF, 3, 1), (CX, 2, 1), (M, 4), (T, 3, 1), (T, 3, 3, 0), (M, 3), (T, 2, 3, 1), (T, 3, 3, 1), (M, 6),
+    (C, 1, 0, 1), (R, 1, 0), (R, 0, 1), (C, 0, 1, 0), (R, 2, 0), (C, 0, 1, 1), (C, 1, 0, 0), (RU, 0, 0),
+    (C, 2, 0, 0), (C, 2, 1, 0), (C, 1, 1, 0), (C, 1, 1, 1), (RD, 0, 0), (R, 1, 1), (Z3, 0), (S2,),
+    (R, 3, 0), (CD, 0, 0), (Z2, 0), (C, 3, 0, 0), (R, 2, 1), (C, 3, 1, 0), (C, 3, 0, 1), (C, 3, 1, 1),
+    (C, 2, 0, 1), (RZ, 1, 0), (R, 3, 1), (RU, 1, 0), (Z3, 1), (RZ, 1, 1), (RU, 1, 1), (RD, 2, 0),
+    (RD, 0, 1), (CD, 2, 0), (Z1, 1), (CU, 0, 0), (C, 2, 1, 1), (RU, 0, 1), (Z1, 0), (RD, 1, 1), (Z2, 1),
+    (K1,), (RV, 0, 0), (RU, 2, 0), (CU, 0, 2), (RD, 3, 0), (RZ, 3, 0), (RD, 2, 1), (RZ, 2, 1), (CD, 0, 2),
+    (RZ, 2, 0), (CU, 1, 0), (CD, 1, 0), (CU, 3, 0), (RD, 1, 2), (CD, 1, 2), (Z3, 2), (RU, 1, 2), (CU, 1, 1),
+    (RD, 1, 0), (Z1, 2), (RF, 0, 0), (RZ, 3, 1), (Z2, 2), (Z1, 3), (CU, 0, 1), (Z3, 3), (CX, 0, 1),
+    (CD, 0, 1), (K2,), (RV, 0, 1), (RU, 3, 0), (RF, 2, 0), (CU, 1, 2), (CD, 1, 1), (CD, 2, 1), (RU, 3, 1),
+    (RD, 2, 2), (CU, 2, 1), (CU, 3, 1), (T, 1, 0), (CD, 3, 0), (CX, 1, 1), (T, 1, 1), (RD, 3, 1), (Z2, 3),
+    (T, 3, 0), (RU, 3, 2), (T, 1, 2), (T, 2, 0), (RD, 3, 2), (RU, 2, 2), (T, 0, 3, 0), (K3,), (CU, 2, 0),
+    (CX, 0, 0), (T, 2, 3, 0), (CD, 2, 2), (CX, 2, 0), (RF, 1, 1), (RV, 0, 2), (RV, 0, 3), (RU, 2, 1),
+    (RF, 3, 0), (RF, 1, 0), (T, 0, 0), (CX, 1, 0), (CD, 3, 1), (T, 2, 1), (RF, 2, 1), (RF, 3, 1), (T, 0, 1),
+    (T, 3, 2), (CU, 3, 2), (CU, 2, 2), (CD, 3, 2), (CX, 3, 0), (M, 2), (T, 0, 2), (T, 3, 1), (M, 0),
+    (T, 1, 3, 1), (T, 2, 2), (CX, 2, 1), (M, 1), (T, 3, 3, 0), (T, 1, 3, 0), (M, 3), (T, 0, 3, 1),
+    (CX, 3, 1), (T, 3, 3, 1), (M, 6), (T, 2, 3, 1), (M, 4), (M, 5),
 )
 
 
@@ -383,11 +383,11 @@
     means[...] = sums[:64, :128] / (sums[:64, 128:] + 1.0)
     writes = [pltpu.make_async_copy(means, means_hbm, sems.at[0])]
     writes[0].start()
-    for i in range(2):
-        at = pl.ds(i * half, half)
+    for i in range(rows // 256):
+        at = pl.ds(i * 256, 256)
         left = rows_of(rp, LAST, at)
-        for j in range(half // 256):
-            to = pl.ds(j * 256, 256)
+        for j in range(half // 1024):
+            to = pl.ds(j * 1024, 1024)
             out[at, to] = (acc[at, to] + over_rows(left, last[:, to])) / float(total)
             n = len(writes)
             writes.append(pltpu.make_async_copy(out.at[at, to], gram_hbm.at[at, to], sems.at[n]))

time: 60.1 us -> 59.9 us (level)
  no operation moved by 1% of the time
where the time goes in v5:
time: 59.9 us; the launch traced here: 59.7 us
  Pallas kernels  59.1 us (99%)
  between operations  0.64 us (1%)
    pallas_call x1, Pallas kernels, body(): pl.pallas_call(exchange, out_shape=(pltpu.VMEM((block, half), jnp.float32...  55.4 us
    pallas_call x1, Pallas kernels, body(): pl.pallas_call(finish, out_shape=(jax.ShapeDtypeStruct((block, half), jnp...  3.71 us

profile of v5, /device:TPU:1, one launch (start us, length us, event | category | flops | bytes accessed | tf_op | source)
XLA Modules:
  0.0 59.7 jit_solution(7482831195973632498)
XLA Ops:
  0.6 55.4 %shard_map.59 = (f32[2048,1024]{1,0:T(8,128)S(1)}, f32[128,256]{1,0:T(8,128)S(1)}, bf16[16,2,4,16,2048]{4,3,2,1,0:T(8,128)(2,1)S(1)}, bf16[256,1024]{1,0:T(8,128)(2,1)S(1)}) custom-call(bf16[16,16384]{1,0:T(8,128)(2,1)} %x_hbm.1, s32[1,16]{1,0:T(1,128)} %bitcast.3, s32[1,16]{1,0:T(1,128)} %bitcast.4, f32[1,64]{1,0:T(1,128)} %bitcast.5), custom_call_target="tpu_custom_call" | custom-call | tf_op jit(solution)/shard_map/pallas_call | solution.py:407
  56.0 3.7 %shard_map.60 = (f32[2048,1024]{1,0:T(8,128)}, f32[64,128]{1,0:T(8,128)}) custom-call(f32[2048,1024]{1,0:T(8,128)S(1)} %get-tuple-element.6.acc, f32[128,256]{1,0:T(8,128)S(1)} %get-tuple-element.7.sums, bf16[16,2,4,16,2048]{4,3,2,1,0:T(8,128)(2,1)S(1)} %get-tuple-element.8.rp, bf16[256,1024]{1,0:T(8,128)(2,1)S(1)} %get-tuple-element.9.last), custom_call_target="tpu_custom_call" | custom-call | tf_op jit(solution)/shard_map/pallas_call | solution.py:445

commit v6 on v5

--- a/solution.py
+++ b/solution.py
@@ -30,22 +30,22 @@
 KINDS = range(22)
 R, C, RZ, Z1, Z2, Z3, RU, RD, CU, CD, RF, CX, RV, T, K1, K2, K3, S2, M, OWN, READY, FAR = KINDS
 ORDER = (
-    (C, 1, 0, 1), (R, 1, 0), (R, 0, 1), (C, 0, 1, 0), (R, 2, 0), (C, 0, 1, 1), (C, 1, 0, 0), (RU, 0, 0),
-    (C, 2, 0, 0), (C, 2, 1, 0), (C, 1, 1, 0), (C, 1, 1, 1), (RD, 0, 0), (R, 1, 1), (Z3, 0), (S2,),
-    (R, 3, 0), (CD, 0, 0), (Z2, 0), (C, 3, 0, 0), (R, 2, 1), (C, 3, 1, 0), (C, 3, 0, 1), (C, 3, 1, 1),
-    (C, 2, 0, 1), (RZ, 1, 0), (R, 3, 1), (RU, 1, 0), (Z3, 1), (RZ, 1, 1), (RU, 1, 1), (RD, 2, 0),
-    (RD, 0, 1), (CD, 2, 0), (Z1, 1), (CU, 0, 0), (C, 2, 1, 1), (RU, 0, 1), (Z1, 0), (RD, 1, 1), (Z2, 1),
-    (K1,), (RV, 0, 0), (RU, 2, 0), (CU, 0, 2), (RD, 3, 0), (RZ, 3, 0), (RD, 2, 1), (RZ, 2, 1), (CD, 0, 2),
-    (RZ, 2, 0), (CU, 1, 0), (CD, 1, 0), (CU, 3, 0), (RD, 1, 2), (CD, 1, 2), (Z3, 2), (RU, 1, 2), (CU, 1, 1),
-    (RD, 1, 0), (Z1, 2), (RF, 0, 0), (RZ, 3, 1), (Z2, 2), (Z1, 3), (CU, 0, 1), (Z3, 3), (CX, 0, 1),
-    (CD, 0, 1), (K2,), (RV, 0, 1), (RU, 3, 0), (RF, 2, 0), (CU, 1, 2), (CD, 1, 1), (CD, 2, 1), (RU, 3, 1),
-    (RD, 2, 2), (CU, 2, 1), (CU, 3, 1), (T, 1, 0), (CD, 3, 0), (CX, 1, 1), (T, 1, 1), (RD, 3, 1), (Z2, 3),
-    (T, 3, 0), (RU, 3, 2), (T, 1, 2), (T, 2, 0), (RD, 3, 2), (RU, 2, 2), (T, 0, 3, 0), (K3,), (CU, 2, 0),
-    (CX, 0, 0), (T, 2, 3, 0), (CD, 2, 2), (CX, 2, 0), (RF, 1, 1), (RV, 0, 2), (RV, 0, 3), (RU, 2, 1),
-    (RF, 3, 0), (RF, 1, 0), (T, 0, 0), (CX, 1, 0), (CD, 3, 1), (T, 2, 1), (RF, 2, 1), (RF, 3, 1), (T, 0, 1),
-    (T, 3, 2), (CU, 3, 2), (CU, 2, 2), (CD, 3, 2), (CX, 3, 0), (M, 2), (T, 0, 2), (T, 3, 1), (M, 0),
-    (T, 1, 3, 1), (T, 2, 2), (CX, 2, 1), (M, 1), (T, 3, 3, 0), (T, 1, 3, 0), (M, 3), (T, 0, 3, 1),
-    (CX, 3, 1), (T, 3, 3, 1), (M, 6), (T, 2, 3, 1), (M, 4), (M, 5),
+    (C, 0, 1, 1), (C, 1, 0, 1), (R, 1, 0), (R, 0, 1), (R, 2, 0), (C, 0, 1, 0), (RD, 0, 0), (C, 2, 0, 1),
+    (C, 2, 1, 0), (C, 1, 0, 0), (S2,), (R, 1, 1), (Z2, 0), (C, 1, 1, 1), (C, 2, 1, 1), (C, 3, 1, 0),
+    (RU, 0, 0), (C, 1, 1, 0), (R, 2, 1), (CD, 0, 0), (R, 3, 0), (C, 3, 1, 1), (Z3, 0), (RZ, 1, 0),
+    (C, 2, 0, 0), (RU, 1, 0), (K1,), (R, 3, 1), (C, 3, 0, 0), (RZ, 2, 0), (RD, 0, 1), (C, 3, 0, 1), (Z1, 0),
+    (RU, 0, 1), (RZ, 1, 1), (RV, 0, 0), (RD, 1, 1), (Z2, 1), (Z1, 1), (Z1, 2), (RU, 1, 1), (RD, 1, 0),
+    (CU, 0, 2), (RD, 2, 0), (RU, 3, 0), (CD, 0, 2), (K2,), (RU, 2, 0), (CU, 0, 0), (CU, 1, 0), (Z3, 1),
+    (RZ, 2, 1), (RD, 1, 2), (CD, 2, 0), (Z3, 2), (CU, 0, 1), (Z1, 3), (CU, 2, 0), (RV, 0, 1), (RF, 1, 0),
+    (CD, 1, 1), (Z2, 2), (RU, 2, 1), (CD, 3, 0), (RD, 2, 1), (RU, 3, 1), (CD, 2, 1), (CD, 1, 0), (CU, 1, 1),
+    (RZ, 3, 1), (RU, 1, 2), (CU, 2, 1), (RF, 0, 0), (RZ, 3, 0), (RF, 1, 1), (CX, 0, 1), (CD, 3, 1),
+    (T, 2, 0), (RU, 2, 2), (RD, 2, 2), (CU, 3, 1), (CD, 1, 2), (CU, 3, 0), (RF, 3, 0), (Z3, 3), (CX, 0, 0),
+    (RD, 3, 1), (K3,), (T, 0, 1), (RD, 3, 0), (Z2, 3), (CX, 2, 0), (T, 1, 1), (RV, 0, 2), (CU, 2, 2),
+    (CD, 2, 2), (T, 0, 0), (RV, 0, 3), (CD, 0, 1), (T, 0, 3, 0), (T, 1, 2), (RD, 3, 2), (RU, 3, 2),
+    (T, 1, 0), (T, 1, 3, 1), (RF, 2, 0), (CU, 3, 2), (T, 3, 0), (CD, 3, 2), (T, 1, 3, 0), (CU, 1, 2),
+    (T, 2, 2), (CX, 1, 0), (RF, 2, 1), (T, 2, 1), (M, 0), (T, 0, 2), (CX, 3, 0), (M, 2), (RF, 3, 1),
+    (T, 3, 2), (T, 3, 3, 0), (CX, 1, 1), (CX, 2, 1), (T, 0, 3, 1), (T, 3, 1), (M, 1), (CX, 3, 1),
+    (T, 2, 3, 0), (M, 5), (T, 2, 3, 1), (M, 3), (T, 3, 3, 1), (M, 4), (M, 6),
 )
 
 
@@ -383,8 +383,8 @@
     means[...] = sums[:64, :128] / (sums[:64, 128:] + 1.0)
     writes = [pltpu.make_async_copy(means, means_hbm, sems.at[0])]
     writes[0].start()
-    for i in range(rows // 256):
-        at = pl.ds(i * 256, 256)
+    for i in range(rows // 128):
+        at = pl.ds(i * 128, 128)
         left = rows_of(rp, LAST, at)
         for j in range(half // 1024):
             to = pl.ds(j * 1024, 1024)
@@ -453,7 +453,7 @@
         scratch_shapes=[
             pltpu.VMEM((block, half), jnp.float32),
             pltpu.VMEM((classes, 128), jnp.float32),
-            pltpu.SemaphoreType.DMA((9,)),
+            pltpu.SemaphoreType.DMA((17,)),
         ],
         compiler_params=pltpu.CompilerParams(vmem_limit_bytes=14 * 1024 * 1024),
     )(*parts)

time: 59.9 us -> 59.8 us (level)
  no operation moved by 1% of the time
where the time goes in v6:
time: 59.8 us; the launch traced here: 59.6 us
  Pallas kernels  59 us (99%)
  between operations  0.64 us (1%)
    pallas_call x1, Pallas kernels, body(): pl.pallas_call(exchange, out_shape=(pltpu.VMEM((block, half), jnp.float32...  55.3 us
    pallas_call x1, Pallas kernels, body(): pl.pallas_call(finish, out_shape=(jax.ShapeDtypeStruct((block, half), jnp...  3.71 us

profile of v6, /device:TPU:1, one launch (start us, length us, event | category | flops | bytes accessed | tf_op | source)
XLA Modules:
  0.0 59.6 jit_solution(17613464130571637199)
XLA Ops:
  0.6 55.3 %shard_map.59 = (f32[2048,1024]{1,0:T(8,128)S(1)}, f32[128,256]{1,0:T(8,128)S(1)}, bf16[16,2,4,16,2048]{4,3,2,1,0:T(8,128)(2,1)S(1)}, bf16[256,1024]{1,0:T(8,128)(2,1)S(1)}) custom-call(bf16[16,16384]{1,0:T(8,128)(2,1)} %x_hbm.1, s32[1,16]{1,0:T(1,128)} %bitcast.3, s32[1,16]{1,0:T(1,128)} %bitcast.4, f32[1,64]{1,0:T(1,128)} %bitcast.5), custom_call_target="tpu_custom_call" | custom-call | tf_op jit(solution)/shard_map/pallas_call | solution.py:407
  55.9 3.7 %shard_map.60 = (f32[2048,1024]{1,0:T(8,128)}, f32[64,128]{1,0:T(8,128)}) custom-call(f32[2048,1024]{1,0:T(8,128)S(1)} %get-tuple-element.6.acc, f32[128,256]{1,0:T(8,128)S(1)} %get-tuple-element.7.sums, bf16[16,2,4,16,2048]{4,3,2,1,0:T(8,128)(2,1)S(1)} %get-tuple-element.8.rp, bf16[256,1024]{1,0:T(8,128)(2,1)S(1)} %get-tuple-element.9.last), custom_call_target="tpu_custom_call" | custom-call | tf_op jit(solution)/shard_map/pallas_call | solution.py:445
